TPU v7x, 32 devices: a whole 2x2x4 slice. The times are simulated.
32 devices in a mesh: head: 4 (over y, x), seq: 8 (over z, core).
Axes of the slice: x: 2, y: 2, z: 4, core: 2. Of those that a mesh axis runs over, the one named last changes fastest.
Arguments:
- prompts: bfloat16 [16, 256, 4096], P('seq'), may hold values from -6 to 6
- prompt_len: int32 [16], replicated, may hold values from 32 to 256, as said below
- admitted: int32 [4], replicated, may hold values from -1 to 15, as said below
- cache_len: int32 [4], replicated, may hold values from 256 to 4096, as said below
- cache_kv: bfloat16 [4, 4, 4096, 256], P('head', None, 'seq'), may hold values from -12 to 12
- dec_tokens: bfloat16 [4, 4, 4096], replicated, may hold values from -6 to 6
- w_query: bfloat16 [4096, 4096], P(None, 'head'), may hold values from -0.09375 to 0.09375
- w_key: bfloat16 [4096, 512], P(None, 'head'), may hold values from -0.09375 to 0.09375
- w_value: bfloat16 [4096, 512], P(None, 'head'), may hold values from -0.09375 to 0.09375
- w_out: bfloat16 [4096, 4096], P('head'), may hold values from -0.09375 to 0.09375
- q_gain: float32 [128], replicated, may hold values from 0.25 to 16
- k_gain: float32 [128], replicated, may hold values from 0.25 to 16
Outputs:
- prefill_out: bfloat16 [16, 256, 4096], P('seq', None, 'head')
- handed_kv: bfloat16 [4, 16, 256, 256], P('head', None, 'seq')
- decode_out: bfloat16 [4, 4, 4096], P(None, None, 'head')
Inputs may be any that keep to these rules, and one draw needn't show every extreme that they name: `prompt_len`: some prompt has exactly 256 live tokens. `admitted`: slots with an entry of 0 or more name distinct prompts; in every draw some slot keeps its cache and some slot takes prompt 16 - 1. `cache_len`: some slot has exactly 4096 live positions.
All inputs are finite; a program needn't handle non-finite values.
Results may differ from a plain program's by a relative error of at most 0.02.
The roundings to bfloat16 on the way count: a program that leaves them out, or rounds other values in their place, can miss the bound.
Values may be sent and summed in bfloat16 or wider, within the bound.
No kernel may reach another device: no remote copies, remote signals or barrier semaphores. Data moves between devices by JAX's collectives and lax.ppermute only.
A program may use at most 128 MiB of HBM per device.

v0:
```python
import jax
import jax.numpy as jnp
from jax import lax
from jax.sharding import PartitionSpec as P

D = 4096
HQ = 32
KVH = 4
HD = 128


EPS = 1e-06
THETA = 1000000.0
NEG = -1e30


def combined_all(value, axis, join):
    pieces = jax.tree.map(lambda part: lax.all_gather(part, axis), value)
    head = jax.tree.map(lambda part: part[0], pieces)
    tail = jax.tree.map(lambda part: part[1:], pieces)
    subtotal, _ = lax.scan(lambda subtotal, slab: (join(subtotal, slab), None), head, tail)
    return subtotal


def rotate(values, positions):
    half = values.shape[-1] // 2
    freq = THETA ** (-jnp.arange(half, dtype=jnp.float32) / half)
    angle = positions.astype(jnp.float32)[..., None, None] * freq
    cosine = jnp.cos(angle)
    sine = jnp.sin(angle)
    first = values[..., :half]
    second = values[..., half:]
    return jnp.concatenate(
        [first * cosine - second * sine, second * cosine + first * sine], axis=-1
    )


def normalize(values, gain):
    return values * lax.rsqrt(jnp.mean(values * values, axis=-1, keepdims=True) + EPS) * gain


def combine(first, second):
    top_a, total_a, acc_a = first
    top_b, total_b, acc_b = second
    best = jnp.maximum(top_a, top_b)
    scale_a = jnp.exp(top_a - best)
    scale_b = jnp.exp(top_b - best)
    return (
        best,
        total_a * scale_a + total_b * scale_b,
        acc_a * scale_a[..., None] + acc_b * scale_b[..., None],
    )


def local(
    prompts,
    prompt_len,
    admitted,
    cache_len,
    cache_kv,
    dec_tokens,
    w_query,
    w_key,
    w_value,
    w_out,
    q_gain,
    k_gain,
):
    seq_count = lax.axis_size("seq")
    seq_index = lax.axis_index("seq")
    group = HQ // KVH
    scale = HD ** (-0.5)
    kv_local = w_key.shape[1] // HD
    heads = kv_local * group
    pr_dev, length_p = (prompts.shape[0], prompts.shape[1])
    spots = jnp.arange(length_p, dtype=jnp.int32)
    own_len = lax.dynamic_slice_in_dim(prompt_len, seq_index * pr_dev, pr_dev)
    flat = prompts.reshape(pr_dev * length_p, D)
    query = jnp.dot(flat, w_query, preferred_element_type=jnp.float32).reshape(
        pr_dev, length_p, heads, HD
    )
    key = jnp.dot(flat, w_key, preferred_element_type=jnp.float32).reshape(
        pr_dev, length_p, kv_local, HD
    )
    value = jnp.dot(flat, w_value, preferred_element_type=jnp.float32).reshape(
        pr_dev, length_p, kv_local, HD
    )
    query = rotate(normalize(query, q_gain), spots).astype(jnp.bfloat16)
    key = rotate(normalize(key, k_gain), spots).astype(jnp.bfloat16)
    value = value.astype(jnp.bfloat16)

    def attend(item):
        q_one, k_one, v_one, length = item
        grouped = q_one.reshape(length_p, kv_local, group, HD)
        scores = (
            jnp.einsum("skgd,tkd->kgst", grouped, k_one, preferred_element_type=jnp.float32) * scale
        )
        allowed = (spots[None, :] <= spots[:, None]) & (spots[None, :] < length)
        scores = jnp.where(allowed, scores, NEG)
        weights = jax.nn.softmax(scores, axis=-1).astype(jnp.bfloat16)
        mixed = jnp.einsum("kgst,tkd->skgd", weights, v_one, preferred_element_type=jnp.float32)
        return mixed.reshape(length_p, heads * HD).astype(jnp.bfloat16)

    attn = lax.map(attend, (query, key, value, own_len)).reshape(pr_dev * length_p, heads * HD)
    partial_out = jnp.dot(attn, w_out, preferred_element_type=jnp.float32).reshape(
        pr_dev, length_p, D
    )
    prefill_out = lax.psum_scatter(
        partial_out.astype(jnp.bfloat16), "head", scatter_dimension=2, tiled=True
    )
    rows_each = length_p // seq_count
    kv_all = jnp.concatenate([key, value], axis=-1)
    sending = kv_all.reshape(pr_dev, rows_each, seq_count, kv_local, 2 * HD).transpose(
        3, 0, 1, 2, 4
    )
    handed = lax.all_to_all(sending, "seq", split_axis=3, concat_axis=1, tiled=True)
    handed = handed.reshape(kv_local, pr_dev * seq_count, rows_each, 2 * HD)
    slots = cache_len.shape[0]
    prompt_count = prompt_len.shape[0]
    steps = dec_tokens.shape[0]
    width = cache_kv.shape[2]
    is_new = admitted >= 0
    placed = admitted[:, None] == jnp.arange(prompt_count, dtype=jnp.int32)[None, :]
    new_len = jnp.sum(jnp.where(placed, prompt_len[None, :], 0), axis=1)
    eff_len = jnp.where(is_new, new_len, cache_len)
    order = jnp.arange(steps, dtype=jnp.int32)
    places = eff_len[None, :] + order[:, None]
    rows = dec_tokens.reshape(steps * slots, D)
    dec_query = jnp.dot(rows, w_query, preferred_element_type=jnp.float32).reshape(
        steps, slots, heads, HD
    )
    dec_query = rotate(normalize(dec_query, q_gain), places).astype(jnp.bfloat16)
    dec_key = jnp.dot(rows, w_key, preferred_element_type=jnp.float32).reshape(
        steps, slots, kv_local, HD
    )
    dec_key = rotate(normalize(dec_key, k_gain), places).astype(jnp.bfloat16)
    dec_value = (
        jnp.dot(rows, w_value, preferred_element_type=jnp.float32)
        .reshape(steps, slots, kv_local, HD)
        .astype(jnp.bfloat16)
    )
    one_hot = placed.astype(jnp.bfloat16)
    from_handed = jnp.einsum(
        "rp,kpid->krid", one_hot, handed, preferred_element_type=jnp.float32
    ).astype(jnp.bfloat16)
    head_rows = jnp.where(is_new[None, :, None, None], from_handed, cache_kv[:, :, :rows_each])
    local_kv = jnp.concatenate([head_rows, cache_kv[:, :, rows_each:]], axis=2)
    positions = jnp.arange(width, dtype=jnp.int32) * seq_count + seq_index
    live = positions[None, :] < eff_len[:, None]
    grouped = dec_query.reshape(steps, slots, kv_local, group, HD)
    scores = (
        jnp.einsum(
            "trkgd,krcd->trkgc", grouped, local_kv[..., :HD], preferred_element_type=jnp.float32
        )
        * scale
    )
    mask = live[None, :, None, None, :]
    scores = jnp.where(mask, scores, NEG)
    top = jnp.max(scores, axis=-1)
    expo = jnp.where(mask, jnp.exp(scores - top[..., None]), 0.0)
    total = jnp.sum(expo, axis=-1)
    acc = jnp.einsum("trkgc,krcd->trkgd", expo, local_kv[..., HD:].astype(jnp.float32))
    recent = (
        jnp.einsum("trkgd,urkd->trkgu", grouped, dec_key, preferred_element_type=jnp.float32)
        * scale
    )
    causal = (order[None, :] <= order[:, None])[:, None, None, None, :]
    recent = jnp.where(causal, recent, NEG)
    recent_top = jnp.max(recent, axis=-1)
    recent_expo = jnp.where(causal, jnp.exp(recent - recent_top[..., None]), 0.0)
    recent_total = jnp.sum(recent_expo, axis=-1)
    recent_acc = jnp.einsum("trkgu,urkd->trkgd", recent_expo, dec_value.astype(jnp.float32))
    merged = combined_all((top, total, acc), "seq", combine)
    best, summed, weighted = combine(merged, (recent_top, recent_total, recent_acc))
    mixed = (weighted / summed[..., None]).astype(jnp.bfloat16).reshape(steps * slots, heads * HD)
    part = jnp.dot(mixed, w_out, preferred_element_type=jnp.float32).reshape(steps, slots, D)
    decode_out = lax.psum_scatter(
        part.astype(jnp.bfloat16), "head", scatter_dimension=2, tiled=True
    )
    return (prefill_out, handed, decode_out)


def solution(mesh):
    placed = (
        P("seq", None, None),
        P(),
        P(),
        P(),
        P("head", None, "seq", None),
        P(),
        P(None, "head"),
        P(None, "head"),
        P(None, "head"),
        P("head", None),
        P(),
        P(),
    )
    return jax.shard_map(
        local,
        mesh=mesh,
        in_specs=placed,
        out_specs=(P("seq", None, "head"), P("head", None, "seq", None), P(None, None, "head")),
        check_vma=False,
    )
```

profile of v0, /device:TPU:0, one launch (start us, length us, event | category | flops | bytes accessed | tf_op | source)
XLA Modules:
  0.0 228.4 jit_solution(2026993213564546555)
XLA Ops:
  7.2 3.8 %convolution_convert_fusion.1 = bf16[2,256,128]{2,1,0:T(8,128)(2,1)S(1)} fusion(bf16[2,256,4096]{2,1,0:T(8,128)(2,1)} %param.16, bf16[4096,128]{1,0:T(8,128)(2,1)} %param.24), kind=kOutput, calls=%fused_computation.43 | convolution fusion | flops 536936448 | bytes 5373952 | tf_op jit(solution)/shard_map/dot_general | solution.py:85
  11.1 0.3 multiply_cosine_fusion
  11.4 0.3 copy-done.8
  11.9 3.5 %multiply_reduce_fusion.1 = (f32[512]{0:T(512)S(1)}, f32[512,128]{1,0:T(8,128)S(1)}) fusion(bf16[512,4096]{1,0:T(8,128)(2,1)} %bitcast.263, bf16[4096,128]{1,0:T(8,128)(2,1)S(1)} %copy-done), kind=kOutput, calls=%fused_computation.79 | convolution fusion | flops 537001472 | bytes 5507072 | tf_op jit(solution)/shard_map/dot_general | solution.py:82
  15.6 0.2 subtract_convert_fusion.1
  15.9 0.9 pad_maximum_fusion.2
  16.7 6.3 %all-to-all-start = ((bf16[1,2,32,8,256]{4,2,1,0,3:T(8,128)(2,1)}), bf16[1,2,32,8,256]{4,2,1,0,3:T(8,128)(2,1)S(1)}, u32[]{:S(2)}, u32[]{:S(2)}) async-start(bf16[1,2,32,8,256]{4,2,1,0,3:T(8,128)(2,1)} %pad_maximum_fusion.2), calls=%async_computation.1 | async-start | bytes 524288 | tf_op jit(solution)/shard_map/all_to_all | solution.py:116
  23.1 0.2 reduce-scatter.7.cloned.1.call-start
  23.3 0.5 iota_compare_fusion.2
  23.8 0.9 fusion.40
  24.7 0.7 reshape.512
  25.5 11.9 %copy.120 = bf16[1024,4096]{1,0:T(8,128)(2,1)} copy(bf16[1024,4096]{0,1:T(8,128)(2,1)} %bitcast.248) | data formatting | bytes 16777216 | tf_op jit(solution)/shard_map/dot_general | solution.py:79
  37.4 7.1 %multiply_reduce_fusion.2 = (f32[4,4,8]{1,2,0:T(8,128)}, f32[4,4,8,128]{3,1,2,0:T(4,128)}) fusion(bf16[8,128,4096,1]{2,1,0,3:T(8,128)(2,1)} %bitcast.249, bf16[4,4,4096]{2,1,0:T(4,128)(2,1)S(1)} %copy-done.7), kind=kOutput, calls=%fused_computation.93 | convolution fusion | flops 134250368 | bytes 8585728 | tf_op jit(solution)/shard_map/dot_general | solution.py:129
  44.5 5.1 %multiply_reduce_fusion = (f32[2,256,8]{1,2,0:T(8,128)}, f32[2,256,8,128]{1,3,2,0:T(8,128)S(1)}) fusion(bf16[8,128,4096,1]{2,1,0,3:T(8,128)(2,1)S(1)} %bitcast.250, bf16[2,256,4096]{2,1,0:T(8,128)(2,1)S(1)} %copy-done.20), kind=kOutput, calls=%fused_computation.40 | convolution fusion | flops 4296011776 | bytes 14696448 | tf_op jit(solution)/shard_map/dot_general | solution.py:79
  49.7 0.6 dynamic_slice.29
  50.3 0.2 select_reduce_fusion
  50.5 0.6 copy-done.12
  51.2 0.8 multiply_cosine_fusion.2
  52.0 1.3 multiply_reduce_fusion.3
  53.3 0.7 rsqrt.43
  53.9 0.8 copy.96
  54.7 0.7 fusion.79
  55.4 1.3 fusion.84
  56.8 0.7 add_rsqrt_fusion.1
  57.5 1.0 multiply_multiply_fusion
  58.6 0.3 subtract_convert_fusion
  58.9 0.4 copy-done.10
  59.4 10.3 %while.27 = (s32[]{:T(128)}, bf16[2,256,1024]{1,2,0:T(8,128)(2,1)}, bf16[2,256,1,128]{3,1,0,2:T(8,128)(2,1)}, s32[2]{0:T(128)}, bf16[2,256,1,128]{3,1,2,0:T(8,12...) while((s32[]{:T(128)}, bf16[2,256,1024]{1,2,0:T(8,128)(2,1)}, ...), condition=%wide.region_5.6_spmd.clone.clone, body=%wide.region_2.5_spmd.clone.clone.sunk | while | flops 273019136 | bytes 17606336 | solution.py:104
  59.4 1.3 dynamic_slice.75
  60.7 0.6 iota_compare_fusion.5
  61.5 0.5 fusion.122
  61.9 0.3 fusion.123
  62.3 0.5 convolution_convert_fusion.5
  62.9 0.7 copy-done.22
  63.6 1.0 copy-done.23
  64.6 1.2 dynamic_slice.75
  65.8 0.6 iota_compare_fusion.5
  66.5 0.5 fusion.122
  67.0 0.3 fusion.123
  67.4 0.5 convolution_convert_fusion.5
  68.0 0.7 copy-done.22
  68.7 1.0 copy-done.23
  69.7 1.0 multiply_multiply_fusion.2
  70.7 0.8 subtract_convert_fusion.2
  71.6 1.0 fusion.98
  72.6 0.7 fusion.63
  73.5 0.3 fusion.42
  73.8 0.4 fusion.97
  74.2 0.3 convolution_bitcast_fusion.1
  74.5 0.2 fusion.53
  74.7 14.3 %all-gather.1 = f32[32,4,8]{2,1,0:T(4,128)S(1)} all-gather(f32[4,4,8]{2,1,0:T(4,128)S(1)} %copy.91), channel_id=3, replica_groups=mesh['head'=4,'seq'=8] {'seq'}, dimensions={0}, use_global_device_ids=true | all-gather | bytes 4608 | tf_op jit(solution)/shard_map/all_gather | solution.py:18
  89.0 13.9 %all-gather = f32[32,4,8]{2,1,0:T(4,128)S(1)} all-gather(f32[4,4,8]{2,1,0:T(4,128)S(1)} %copy.90), channel_id=2, replica_groups=mesh['head'=4,'seq'=8] {'seq'}, dimensions={0}, use_global_device_ids=true | all-gather | bytes 4608 | tf_op jit(solution)/shard_map/all_gather | solution.py:18
  102.9 14.9 %all-gather.2 = f32[32,4,1,8,128]{4,3,0,1,2:T(8,128)S(1)} all-gather(f32[4,4,1,8,128]{4,3,0,1,2:T(8,128)S(1)} %convolution_bitcast_fusion.1), channel_id=4, replica_groups=mesh['head'=4,'seq'=8] {'seq'}, dimensions={0}, use_global_device_ids=true | all-gather | bytes 589824 | tf_op jit(solution)/shard_map/all_gather | solution.py:18
  117.9 1.4 while.26
  119.4 0.3 fusion.38
  119.7 4.7 %fusion.26 = bf16[4,4,4096]{2,1,0:T(4,128)(2,1)S(1)} fusion(bf16[1024,4096]{1,0:T(8,128)(2,1)} %param.25, bf16[4,4,1024]{2,0,1:T(4,128)(2,1)S(1)} %dot_general.71), kind=kOutput, calls=%fused_computation.36 | convolution fusion | flops 134283264 | bytes 8552448 | tf_op jit(solution)/shard_map/dot_general | solution.py:176
  124.4 4.8 %copy.118 = bf16[4,4,4096]{1,0,2:T(4,128)(2,1)} copy(bf16[4,4,4096]{2,1,0:T(4,128)(2,1)S(1)} %fusion.26) | data formatting | bytes 262144
  129.1 6.1 %reshape.548 = bf16[4096,16]{1,0:T(8,128)(2,1)} reshape(bf16[4096,4,4]{2,1,0:T(4,128)(2,1)} %bitcast.246) | data formatting | bytes 262144
  135.4 9.5 %fusion.23 = bf16[2,256,4096]{2,1,0:T(8,128)(2,1)} fusion(bf16[2,256,1024]{1,2,0:T(8,128)(2,1)S(1)} %copy-done.24, bf16[1024,4096]{1,0:T(8,128)(2,1)} %param.25), kind=kOutput, calls=%fused_computation.35 | convolution fusion | flops 4297064448 | bytes 13631488 | tf_op jit(solution)/shard_map/dot_general | solution.py:105
  144.9 19.4 %reduce-scatter.7.cloned.1.call-done = bf16[1024,16]{1,0:T(8,128)(2,1)} async-done(((bf16[4096,16]{1,0:T(8,128)(2,1)}), bf16[1024,16]{1,0:T(8,128)(2,1)}) %reduce-scatter.7.cloned.1.call-update) | async-done | bytes 32784
  164.4 2.1 reshape.549
  166.4 1.3 copy.119
  167.7 53.2 %reduce-scatter.5.cloned.1.call-done = bf16[2,256,1024]{2,1,0:T(8,128)(2,1)} async-done(((bf16[2,256,4096]{2,1,0:T(8,128)(2,1)}), bf16[2,256,1024]{2,1,0:T(8,128)(2,1)}) %reduce-scatter.5.cloned.1.call-update) | async-done | bytes 1048592 | tf_op jit(solution)/shard_map/reduce_scatter | solution.py:108
  220.8 0.7 copy.185
  (129 shorter events, 3.0 us)
Async XLA Ops:
  7.2 4.7 %copy-start = (bf16[4096,128]{1,0:T(8,128)(2,1)S(1)}, bf16[4096,128]{1,0:T(8,128)(2,1)}, u32[]{:S(2)}) copy-start(bf16[4096,128]{1,0:T(8,128)(2,1)} %param.23) | copy-start | bytes 3145732
  7.2 44.0 %copy-start.11 = (f32[64]{0:T(128)}, f32[64]{0:T(128)S(1)}, u32[]{:S(2)}) copy-start(f32[64]{0:T(128)S(1)} %multiply_power_fusion) | copy-start | bytes 772
  11.0 0.6 copy-start.8
  11.7 3.7 %copy-start.3 = (f32[256,64]{0,1:T(8,128)}, f32[256,64]{0,1:T(8,128)S(1)}, u32[]{:S(2)}) copy-start(f32[256,64]{0,1:T(8,128)S(1)} %get-tuple-element.202) | copy-start | bytes 196612
  11.7 3.8 %copy-start.5 = (f32[256,64]{0,1:T(8,128)}, f32[256,64]{0,1:T(8,128)S(1)}, u32[]{:S(2)}) copy-start(f32[256,64]{0,1:T(8,128)S(1)} %get-tuple-element.203) | copy-start | bytes 196612
  11.9 3.6 %copy-start.14 = (f32[128]{0:T(128)S(1)}, f32[128]{0:T(128)}, u32[]{:S(2)}) copy-start(f32[128]{0:T(128)} %param.27) | copy-start | bytes 1540
  15.4 8.4 %copy-start.7 = (bf16[4,4,4096]{2,1,0:T(4,128)(2,1)S(1)}, bf16[4,4,4096]{2,1,0:T(4,128)(2,1)}, u32[]{:S(2)}) copy-start(bf16[4,4,4096]{2,1,0:T(4,128)(2,1)} %param.21) | copy-start | bytes 393220
  15.5 8.4 %copy-start.21 = (bf16[4096,128]{1,0:T(8,128)(2,1)S(1)}, bf16[4096,128]{1,0:T(8,128)(2,1)}, u32[]{:S(2)}) copy-start(bf16[4096,128]{1,0:T(8,128)(2,1)} %param.24) | copy-start | bytes 3145732
  16.7 56.8 %all-to-all-start = ((bf16[1,2,32,8,256]{4,2,1,0,3:T(8,128)(2,1)}), bf16[1,2,32,8,256]{4,2,1,0,3:T(8,128)(2,1)S(1)}, u32[]{:S(2)}, u32[]{:S(2)}) async-start(bf16[1,2,32,8,256]{4,2,1,0,3:T(8,128)(2,1)} %pad_maximum_fusion.2), calls=%async_computation.1 | async-start | bytes 524288 | tf_op jit(solution)/shard_map/all_to_all | solution.py:116
  23.1 141.3 %reduce-scatter.7.cloned.1.call-start = ((), (), s32[]{:S(2)}) async-start(), calls=%async_computation.4 | async-start | bytes 1310720
  37.4 7.1 %copy-start.1 = (bf16[1024,4096]{1,0:T(8,128)(2,1)S(1)}, bf16[1024,4096]{1,0:T(8,128)(2,1)}, u32[]{:S(2)}) copy-start(bf16[1024,4096]{1,0:T(8,128)(2,1)} %copy.120) | copy-start | bytes 25165828
  37.4 7.1 %copy-start.20 = (bf16[2,256,4096]{2,1,0:T(8,128)(2,1)S(1)}, bf16[2,256,4096]{2,1,0:T(8,128)(2,1)}, u32[]{:S(2)}) copy-start(bf16[2,256,4096]{2,1,0:T(8,128)(2,1)} %param.16) | copy-start | bytes 12582916
  44.5 5.2 %copy-start.25 = (s32[16]{0:T(128)S(1)}, s32[16]{0:T(128)}, u32[]{:S(2)}) copy-start(s32[16]{0:T(128)} %param.17) | copy-start | bytes 196
  44.5 5.7 %copy-start.17 = (s32[4]{0:T(128)S(1)}, s32[4]{0:T(128)}, u32[]{:S(2)}) copy-start(s32[4]{0:T(128)} %param.18) | copy-start | bytes 52
  44.5 5.9 %copy-start.16 = (s32[4]{0:T(128)S(1)}, s32[4]{0:T(128)}, u32[]{:S(2)}) copy-start(s32[4]{0:T(128)} %param.19) | copy-start | bytes 52
  50.5 0.6 copy-start.12
  57.5 1.0 copy-start.4
  57.5 1.1 copy-start.6
  58.6 0.7 copy-start.10
  59.4 14.0 %copy-start.2 = (bf16[1,4,512,256]{3,2,1,0:T(8,128)(2,1)S(1)}, bf16[1,4,512,256]{3,2,1,0:T(8,128)(2,1)}, u32[]{:S(2)}) copy-start(bf16[1,4,512,256]{3,2,1,0:T(8,128)(2,1)} %param.20) | copy-start | bytes 3145732
  61.4 0.9 copy-start.9
  62.3 1.2 copy-start.22
  63.6 1.0 copy-start.23
  66.5 0.9 copy-start.9
  67.4 1.2 copy-start.22
  68.7 1.0 copy-start.23
  69.7 3.7 %copy-start.18 = (s32[4]{0:T(128)S(1)}, s32[4]{0:T(128)}, u32[]{:S(2)}) copy-start(s32[4]{0:T(128)} %param.18) | copy-start | bytes 52
  69.7 3.8 %copy-start.13 = (s32[4]{0:T(128)S(1)}, s32[4]{0:T(128)}, u32[]{:S(2)}) copy-start(s32[4]{0:T(128)} %copy-done.12) | copy-start | bytes 52
  69.7 3.8 %slice-start = ((bf16[1,4,512,256]{3,2,1,0:T(8,128)(2,1)}), bf16[1,4,32,256]{3,2,1,0:T(8,128)(2,1)S(1)}, s32[]{:S(2)}) async-start(bf16[1,4,512,256]{3,2,1,0:T(8,128)(2,1)} %param.20), calls=%async_computation.5 | async-start | bytes 131072 | tf_op jit(solution)/shard_map/slice | solution.py:146
  70.7 2.9 %copy-start.19 = (s32[4]{0:T(128)S(1)}, s32[4]{0:T(128)}, u32[]{:S(2)}) copy-start(s32[4]{0:T(128)} %param.18) | copy-start | bytes 52
  74.7 44.7 %copy-start.15 = (pred[4,4]{1,0:T(4,128)(4,1)S(1)}, pred[4,4]{1,0:T(4,128)(4,1)}, u32[]{:S(2)}) copy-start(pred[4,4]{1,0:T(4,128)(4,1)} %iota_compare_fusion.2) | copy-start | bytes 52
  74.7 44.7 %copy-start.26 = (bf16[4,4,128,1]{2,1,0,3:T(4,128)(2,1)S(1)}, bf16[4,4,128,1]{2,1,0,3:T(4,128)(2,1)}, u32[]{:S(2)}) copy-start(bf16[4,4,128,1]{2,1,0,3:T(4,128)(2,1)} %fusion.40) | copy-start | bytes 12292
  129.1 6.2 %copy-start.24 = (bf16[2,256,1024]{1,2,0:T(8,128)(2,1)S(1)}, bf16[2,256,1024]{1,2,0:T(8,128)(2,1)}, u32[]{:S(2)}) copy-start(bf16[2,256,1024]{1,2,0:T(8,128)(2,1)} %get-tuple-element.82) | copy-start | bytes 3145732
  135.3 85.5 %reduce-scatter.5.cloned.1.call-start = ((), (), s32[]{:S(2)}) async-start(), calls=%async_computation.3 | async-start | bytes 5242880 | tf_op jit(solution)/shard_map/reduce_scatter | solution.py:108
Sparse Core Ops, SparseCore 0:
  135.4 28.8 reduce-scatter.6
  168.2 52.6 reduce-scatter.4
where the time goes:
time: 230 us; the launch traced here: 228 us
  waiting for transfers between devices  72.6 us (32%)
  blocking collectives  43.1 us (19%)
  matrix products  40.1 us (17%)
  local copies, waits for them, and re-layouts  37.5 us (16%)
  between operations  14.6 us (6%)
  other arithmetic  13.5 us (6%)
  starting transfers between devices  6.58 us (3%)
    reduce_scatter x1, waiting for transfers between devices, local(): lax.psum_scatter(partial_out.astype(jnp.bfloat16), 'head', scatter_dimens...  53.2 us
    all_gather x3, blocking collectives, combined_all(): pieces = jax.tree.map(lambda part: lax.all_gather(part, axis), value)  43.1 us
    unnamed x3, waiting for transfers between devices  19.5 us
    unnamed x53, local copies, waits for them, and re-layouts  16.3 us
    dot_general x1, local copies, waits for them, and re-layouts, local(): jnp.dot(flat, w_query, preferred_element_type=jnp.float32)  11.9 us
    dot_general x1, matrix products, local(): jnp.dot(attn, w_out, preferred_element_type=jnp.float32)  9.54 us
    dot_general x1, matrix products, local(): jnp.dot(rows, w_query, preferred_element_type=jnp.float32)  7.1 us
    all_to_all x1, starting transfers between devices, local(): lax.all_to_all(sending, 'seq', split_axis=3, concat_axis=1, tiled=True)  6.32 us
  transfers between devices with their start and end apart: 3, of which 2 were waited for; matrix products, arithmetic and copies ran while one was open for 25% of the time, Pallas kernels for 0%

commit v1 on v0

v1 whole, which is shorter than its diff:
```python
import functools

import jax
import jax.numpy as jnp
import numpy as np
from jax import lax
from jax.experimental import pallas as pl
from jax.experimental.pallas import tpu as pltpu
from jax.sharding import PartitionSpec as P

HD = 128
EPS = 1e-06
THETA = 1000000.0
NEG = -1e30
LOG2E = 1.4426950408889634
SCALE = HD**-0.5
C2 = SCALE * LOG2E
BF = jnp.bfloat16
F32 = jnp.float32
ANY = pl.BlockSpec(memory_space=pl.ANY)
VM = pl.BlockSpec(memory_space=pltpu.VMEM)
SM = pl.BlockSpec(memory_space=pltpu.SMEM)
MIB = 1024 * 1024


def frequencies():
    half = HD // 2
    freq = np.float32(THETA) ** (-np.arange(half, dtype=np.float32) / np.float32(half))
    return freq.astype(np.float32)


def prompt_table(length):
    angle = np.arange(length, dtype=np.float32)[:, None] * frequencies()[None, :]
    cosine, sine = np.cos(angle), np.sin(angle)
    return np.concatenate([cosine, cosine, -sine, sine], axis=1).astype(np.float32)


def dot(a, b):
    return jnp.dot(a, b, preferred_element_type=F32)


def dot_nt(a, b):
    return lax.dot_general(a, b, (((1,), (1,)), ((), ())), preferred_element_type=F32)


def norm(values, gain):
    square = jnp.mean(values * values, axis=-1, keepdims=True)
    return values * lax.rsqrt(square + EPS) * gain


def rope(values, cos2, sin2):
    return values * cos2 + pltpu.roll(values, HD // 2, 1) * sin2


def effective_lengths(plen, adm, clen, slots):
    out = []
    for r in range(slots):
        taken = adm[r]
        out.append(jnp.where(taken >= 0, plen[jnp.maximum(taken, 0)], clen[r]))
    return out


def by_slot(index, values):
    result = jnp.full(index.shape, values[0])
    for r in range(1, len(values)):
        result = jnp.where(index == r, values[r], result)
    return result


def prefill_kernel(which, dec_rows, slots, n_head, *refs):
    it = iter(refs)
    plen, adm, clen = next(it), next(it), next(it)
    x_hbm = next(it)
    dec_hbm = next(it) if dec_rows else None
    wq_hbm, wk_hbm, wv_hbm, wo_hbm = next(it), next(it), next(it), next(it)
    qg, kg, table, freq = next(it), next(it), next(it), next(it)
    send_a, send_b, attn, kv_out = next(it), next(it), next(it), next(it)
    if dec_rows:
        dq_out, dkv_out = next(it), next(it)
    x_v, wkv_v, wq_v, wo_v, x_sem, wkv_sem, wq_sem, wo_sem = it

    rows, width = kv_out.shape[0], x_hbm.shape[2]
    tiles = wq_v.shape[0]
    nb = width // n_head
    hb = nb // 2
    head = lax.axis_index("head")
    flip_x = head + 1 - 2 * lax.rem(head, 2)
    flip_y = lax.rem(head + 2, 4)
    flip_xy = 3 - head

    copies = []
    copies.append(pltpu.make_async_copy(x_hbm.at[which], x_v.at[pl.ds(0, rows)], x_sem.at[0]))
    if dec_rows:
        copies.append(
            pltpu.make_async_copy(dec_hbm, x_v.at[pl.ds(rows, dec_rows)], x_sem.at[1])
        )
    copies.append(pltpu.make_async_copy(wk_hbm, wkv_v.at[:, pl.ds(0, HD)], wkv_sem.at[0]))
    copies.append(pltpu.make_async_copy(wv_hbm, wkv_v.at[:, pl.ds(HD, HD)], wkv_sem.at[1]))
    q_copies = [
        pltpu.make_async_copy(
            wq_hbm.at[:, pl.ds(j * 2 * HD, 2 * HD)], wq_v.at[j], wq_sem.at[j]
        )
        for j in range(tiles)
    ]
    offsets = [
        flip_xy * nb,
        flip_xy * nb + hb,
        flip_x * nb,
        flip_y * nb + hb,
    ]
    o_copies = [
        pltpu.make_async_copy(
            wo_hbm.at[:, pl.ds(pl.multiple_of(offset, hb), hb)], wo_v.at[j], wo_sem.at[j]
        )
        for j, offset in enumerate(offsets)
    ]
    for copy in copies:
        copy.start()
    later = q_copies + o_copies
    ahead = 2
    for copy in later[:ahead]:
        copy.start()

    length = plen[lax.axis_index("seq") * x_hbm.shape[0] + which]
    row_at = lax.broadcasted_iota(jnp.int32, (rows, rows), 0)
    col_at = lax.broadcasted_iota(jnp.int32, (rows, rows), 1)
    bias = jnp.where((col_at <= row_at) & (col_at < length), 0.0, NEG).astype(F32)
    cos2, sin2 = table[:, :HD], table[:, HD:]
    if dec_rows:
        eff = effective_lengths(plen, adm, clen, slots)
        row = lax.broadcasted_iota(jnp.int32, (dec_rows, HD), 0)
        places = by_slot(lax.rem(row, slots), eff) + row // slots
        angle = places.astype(F32) * freq[...]
        lane = lax.broadcasted_iota(jnp.int32, (dec_rows, HD), 1)
        dcos2 = jnp.cos(angle)
        dsin2 = jnp.where(lane < HD // 2, -1.0, 1.0) * jnp.sin(angle)

    for copy in copies:
        copy.wait()
    kv = dot(x_v[...], wkv_v[...])
    key = rope(norm(kv[:rows, :HD], kg[...]), cos2, sin2).astype(BF)
    value = kv[:rows, HD:].astype(BF)
    kv_out[:, :HD] = key
    kv_out[:, HD:] = value
    if dec_rows:
        dkv_out[:, :HD] = rope(norm(kv[rows:, :HD], kg[...]), dcos2, dsin2).astype(BF)
        dkv_out[:, HD:] = kv[rows:, HD:].astype(BF)

    for j in range(tiles):
        q_copies[j].wait()
        if j + ahead < len(later):
            later[j + ahead].start()
        projected = dot(x_v[...], wq_v[j])
        for i in range(2):
            h = 2 * j + i
            piece = projected[:, i * HD : (i + 1) * HD]
            query = rope(norm(piece[:rows], qg[...]), cos2, sin2).astype(BF)
            if dec_rows:
                dq_out[h * dec_rows : (h + 1) * dec_rows, :] = rope(
                    norm(piece[rows:], qg[...]), dcos2, dsin2
                ).astype(BF)
            scores = dot_nt(query, key) + bias
            top = jnp.max(scores, axis=-1, keepdims=True)
            expo = jnp.exp2((scores - top) * C2)
            total = jnp.sum(expo, axis=-1, keepdims=True)
            weights = (expo * (1.0 / total)).astype(BF)
            attn[:, h * HD : (h + 1) * HD] = dot(weights, value).astype(BF)

    for j in range(len(o_copies)):
        o_copies[j].wait()
        if tiles + j + ahead < len(later):
            later[tiles + j + ahead].start()
        part = dot(attn[...], wo_v[j]).astype(BF)
        dest = send_b if j % 2 else send_a
        at = (j // 2) * hb
        dest[:, at : at + hb] = part


def prefill(which, with_dec, n_head, plen, adm, clen, x, dec, wq, wk, wv, wo, qg, kg, table, freq):
    _, rows, width = x.shape
    slots = adm.shape[0]
    dec_rows = dec.shape[0] if with_dec else 0
    local = wq.shape[1]
    tiles = local // (2 * HD)
    nb = width // n_head
    hb = nb // 2
    outs = [
        jax.ShapeDtypeStruct((rows, nb), BF),
        jax.ShapeDtypeStruct((rows, nb), BF),
        jax.ShapeDtypeStruct((rows, local), BF),
        jax.ShapeDtypeStruct((rows, 2 * HD), BF),
    ]
    if with_dec:
        outs += [
            jax.ShapeDtypeStruct((dec_rows * (local // HD), HD), BF),
            jax.ShapeDtypeStruct((dec_rows, 2 * HD), BF),
        ]
    args = [plen, adm, clen, x] + ([dec] if with_dec else []) + [wq, wk, wv, wo, qg, kg, table, freq]
    specs = [SM, SM, SM, ANY] + ([ANY] if with_dec else []) + [ANY] * 4 + [VM] * 4
    total_rows = rows + dec_rows
    flops = 2 * total_rows * width * (local + 2 * HD) + rows * local * width
    return pl.pallas_call(
        functools.partial(prefill_kernel, which, dec_rows, slots, n_head),
        out_shape=outs,
        in_specs=specs,
        out_specs=[VM] * len(outs),
        scratch_shapes=[
            pltpu.VMEM((total_rows, width), BF),
            pltpu.VMEM((width, 2 * HD), BF),
            pltpu.VMEM((tiles, width, 2 * HD), BF),
            pltpu.VMEM((4, local, hb), BF),
            pltpu.SemaphoreType.DMA((2,)),
            pltpu.SemaphoreType.DMA((2,)),
            pltpu.SemaphoreType.DMA((tiles,)),
            pltpu.SemaphoreType.DMA((4,)),
        ],
        compiler_params=pltpu.CompilerParams(vmem_limit_bytes=40 * MIB),
        cost_estimate=pl.CostEstimate(
            flops=flops, bytes_accessed=18 * MIB, transcendentals=local // HD * rows * rows
        ),
        name="prefill_%d" % which,
    )(*args)


def own_kernel(n_head, attn0, attn1, wo_hbm, o_fa, o_fb, o_keep, wo_v, sems):
    width = wo_hbm.shape[1]
    nb = width // n_head
    hb = nb // 2
    head = lax.axis_index("head")
    flip_x = head + 1 - 2 * lax.rem(head, 2)
    flip_y = lax.rem(head + 2, 4)
    offsets = [flip_y * nb, flip_x * nb + hb, head * nb, head * nb + hb]
    copies = [
        pltpu.make_async_copy(
            wo_hbm.at[:, pl.ds(pl.multiple_of(offset, hb), hb)], wo_v.at[j], sems.at[j]
        )
        for j, offset in enumerate(offsets)
    ]
    for copy in copies:
        copy.start()
    for j in range(4):
        copies[j].wait()
        for p, attn in enumerate((attn0, attn1)):
            part = dot(attn[...], wo_v[j])
            if j == 0:
                o_fa[p] = part
            elif j == 1:
                o_fb[p] = part
            else:
                o_keep[p, :, (j - 2) * hb : (j - 1) * hb] = part


def own_parts(n_head, attn0, attn1, wo):
    rows, local = attn0.shape
    width = wo.shape[1]
    nb = width // n_head
    hb = nb // 2
    return pl.pallas_call(
        functools.partial(own_kernel, n_head),
        out_shape=[
            jax.ShapeDtypeStruct((2, rows, hb), F32),
            jax.ShapeDtypeStruct((2, rows, hb), F32),
            jax.ShapeDtypeStruct((2, rows, nb), F32),
        ],
        in_specs=[VM, VM, ANY],
        out_specs=[VM] * 3,
        scratch_shapes=[pltpu.VMEM((4, local, hb), BF), pltpu.SemaphoreType.DMA((4,))],
        compiler_params=pltpu.CompilerParams(vmem_limit_bytes=32 * MIB),
        cost_estimate=pl.CostEstimate(
            flops=2 * rows * local * width, bytes_accessed=9 * MIB, transcendentals=0
        ),
        name="own_parts",
    )(attn0, attn1, wo)


def decode_kernel(n_seq, plen, adm, clen, dq, dkv, cache, *refs):
    kvs, (part, handed) = refs[:-2], refs[-2:]
    seq = lax.axis_index("seq")
    slots, width = cache.shape[0], cache.shape[1]
    queries = dq[...]
    count = queries.shape[0]
    dec_rows = dkv.shape[0]
    rows = kvs[0].shape[0]
    each = rows // n_seq

    row = lax.rem(lax.broadcasted_iota(jnp.int32, (count, 1), 0), dec_rows)
    slot, step = lax.rem(row, slots), row // slots
    taken = by_slot(slot, [adm[r] for r in range(slots)])
    scores, masks, values = [], [], []
    at = lax.broadcasted_iota(jnp.int32, (1, width), 1) * n_seq + seq
    for r in range(slots):
        limit = jnp.where(adm[r] >= 0, 0, clen[r])
        masks.append((slot == r) & (at < limit))
        scores.append(dot_nt(queries, cache[r, :, :HD]))
        values.append(cache[r, :, HD:])
    spot = lax.broadcasted_iota(jnp.int32, (1, rows), 1)
    for p, kv in enumerate(kvs):
        prompt = seq * len(kvs) + p
        masks.append((taken == prompt) & (spot < plen[prompt]))
        scores.append(dot_nt(queries, kv[:, :HD]))
        values.append(kv[:, HD:])
    other = lax.broadcasted_iota(jnp.int32, (1, dec_rows), 1)
    first = jnp.where(seq == 0, 1, 0)
    masks.append(
        (lax.rem(other, slots) == slot) & (other // slots <= step) & (first + 0 * other > 0)
    )
    scores.append(dot_nt(queries, dkv[:, :HD]))
    values.append(dkv[:, HD:])

    top = jnp.full((count, 1), NEG, F32)
    scores = [jnp.where(mask, score, NEG) for mask, score in zip(masks, scores)]
    for score in scores:
        top = jnp.maximum(top, jnp.max(score, axis=-1, keepdims=True))
    total = jnp.zeros((count, 1), F32)
    acc = jnp.zeros((count, HD), F32)
    for mask, score, value in zip(masks, scores, values):
        expo = jnp.where(mask, jnp.exp2((score - top) * C2), 0.0)
        total = total + jnp.sum(expo, axis=-1, keepdims=True)
        acc = acc + dot(expo.astype(BF), value)
    some = total > 0.0
    safe = jnp.where(some, total, 1.0)
    part[:count, :] = acc * (1.0 / safe)
    level = jnp.where(some, top * C2 + jnp.log2(safe), NEG)
    eye = lax.broadcasted_iota(jnp.int32, (count, count), 0) == lax.broadcasted_iota(
        jnp.int32, (count, count), 1
    )
    part[count : count + 1, :] = jnp.sum(jnp.where(eye, level, 0.0), axis=0, keepdims=True)

    new = lax.broadcasted_iota(jnp.int32, (rows, rows), 0)
    old = lax.broadcasted_iota(jnp.int32, (rows, rows), 1)
    move = jnp.where(old == lax.rem(new, each) * n_seq + new // each, 1.0, 0.0).astype(BF)
    for p, kv in enumerate(kvs):
        handed[p] = dot(move, kv[...]).astype(BF)


def decode_attention(n_seq, plen, adm, clen, dq, dkv, cache, kvs):
    count = dq.shape[0]
    rows = kvs[0].shape[0]
    return pl.pallas_call(
        functools.partial(decode_kernel, n_seq),
        out_shape=[
            jax.ShapeDtypeStruct((count + 8, HD), F32),
            jax.ShapeDtypeStruct((len(kvs), rows, 2 * HD), BF),
        ],
        in_specs=[SM] * 3 + [VM] * (3 + len(kvs)),
        out_specs=[VM] * 2,
        compiler_params=pltpu.CompilerParams(vmem_limit_bytes=32 * MIB),
        cost_estimate=pl.CostEstimate(
            flops=400 * MIB, bytes_accessed=2 * MIB, transcendentals=count * 2600
        ),
        name="decode_attention",
    )(plen, adm, clen, dq, dkv, cache, *kvs)


def joined(bit, mine, other):
    count = mine.shape[0] - 8
    swap = lax.rem(lax.axis_index("seq") // bit, 2) == 1
    one, two = mine[...], other[...]
    low = jnp.where(swap, two, one)
    high = jnp.where(swap, one, two)
    eye = lax.broadcasted_iota(jnp.int32, (count, count), 0) == lax.broadcasted_iota(
        jnp.int32, (count, count), 1
    )

    def column(row):
        return jnp.sum(jnp.where(eye, row, 0.0), axis=1, keepdims=True)

    row_a, row_b = low[count : count + 1, :], high[count : count + 1, :]
    best = jnp.maximum(row_a, row_b)
    scale_a, scale_b = jnp.exp2(row_a - best), jnp.exp2(row_b - best)
    total = scale_a + scale_b
    inverse = 1.0 / total
    mixed = low[:count] * column(scale_a * inverse) + high[:count] * column(scale_b * inverse)
    return mixed, best + jnp.log2(total)


def join_kernel(bit, mine, other, out):
    count = mine.shape[0] - 8
    mixed, level = joined(bit, mine, other)
    out[:count, :] = mixed
    out[count : count + 1, :] = level


def join(bit, mine, other):
    return pl.pallas_call(
        functools.partial(join_kernel, bit),
        out_shape=jax.ShapeDtypeStruct(mine.shape, F32),
        in_specs=[VM, VM],
        out_specs=VM,
        name="join_%d" % bit,
    )(mine, other)


def decode_out_kernel(bit, n_head, mine, other, wo, *outs):
    count = mine.shape[0] - 8
    rows = outs[0].shape[0]
    nb = outs[0].shape[1]
    mixed, _ = joined(bit, mine, other)
    mixed = mixed.astype(BF)
    flat = jnp.concatenate([mixed[i * rows : (i + 1) * rows] for i in range(count // rows)], axis=1)
    head = lax.axis_index("head")
    for d in range(n_head):
        dest = head + 1 - 2 * lax.rem(head, 2) if d == 1 else lax.rem(head + 2, 4)
        if d == 0:
            dest = head
        elif d == 3:
            dest = 3 - head
        at = pl.multiple_of(dest * nb, nb)
        outs[d][...] = dot(flat, wo[:, pl.ds(at, nb)]).astype(BF)


def decode_project(bit, n_head, dec_rows, mine, other, wo):
    local, width = wo.shape
    nb = width // n_head
    return pl.pallas_call(
        functools.partial(decode_out_kernel, bit, n_head),
        out_shape=[jax.ShapeDtypeStruct((dec_rows, nb), BF)] * n_head,
        in_specs=[VM] * 3,
        out_specs=[VM] * n_head,
        compiler_params=pltpu.CompilerParams(vmem_limit_bytes=32 * MIB),
        cost_estimate=pl.CostEstimate(
            flops=2 * 256 * local * width, bytes_accessed=8 * MIB, transcendentals=0
        ),
        name="decode_project",
    )(mine, other, wo)


def local(
    prompts, prompt_len, admitted, cache_len, cache_kv, dec_tokens, w_query, w_key, w_value, w_out, q_gain, k_gain
):
    n_seq = lax.axis_size("seq")
    n_head = lax.axis_size("head")
    pr_dev, rows, width = prompts.shape
    steps, slots, _ = dec_tokens.shape
    nb = width // n_head
    hb = nb // 2
    qg, kg = q_gain.reshape(1, HD), k_gain.reshape(1, HD)
    table = jnp.asarray(prompt_table(rows))
    freq = jnp.asarray(np.tile(frequencies(), 2)[None, :])
    dec = dec_tokens.reshape(steps * slots, width)
    scalars = (prompt_len, admitted, cache_len)
    weights = (w_query, w_key, w_value, w_out, qg, kg, table, freq)

    across_x = [(i, i ^ 1) for i in range(n_head)]
    across_y = [(i, i ^ 2) for i in range(n_head)]
    across_xy = [(i, i ^ 3) for i in range(n_head)]

    def head_move(value, pairs):
        return lax.ppermute(value, "head", pairs)

    got, attns, kvs = [], [], []
    for p in range(pr_dev):
        last = p == pr_dev - 1
        out = prefill(p, last, n_head, *scalars, prompts, dec, *weights)
        got.append((head_move(out[0], across_x), head_move(out[1], across_y)))
        attns.append(out[2])
        kvs.append(out[3])
    dq, dkv = out[4], out[5]
    own_fa, own_fb, own_keep = own_parts(n_head, *attns, w_out)

    part, handed = decode_attention(n_seq, *scalars, dq, dkv, cache_kv[0], kvs)
    bit = 1
    while bit < n_seq:
        other = lax.ppermute(part, "seq", [(i, i ^ bit) for i in range(n_seq)])
        if 2 * bit < n_seq:
            part = join(bit, part, other)
        else:
            pieces = decode_project(bit, n_head, steps * slots, part, other, w_out)
        bit *= 2
    total = pieces[0].astype(F32)
    for piece, pairs in zip(pieces[1:], (across_x, across_y, across_xy)):
        total = total + head_move(piece, pairs).astype(F32)
    decode_out = total.astype(BF).reshape(steps, slots, nb)

    each = rows // n_seq
    sending = handed.reshape(pr_dev, n_seq, each, 2 * HD)
    handed = lax.all_to_all(sending, "seq", split_axis=1, concat_axis=0, tiled=True)
    handed = handed.reshape(1, pr_dev * n_seq, each, 2 * HD)

    finals = []
    for p in range(pr_dev):
        a, b = got[p]
        a, b = a.astype(F32), b.astype(F32)
        on_a = head_move((own_fa[p] + a[:, :hb]).astype(BF), across_y)
        on_b = head_move((own_fb[p] + b[:, :hb]).astype(BF), across_x)
        finals.append(
            jnp.concatenate(
                [
                    own_keep[p, :, :hb] + a[:, hb:] + on_a.astype(F32),
                    own_keep[p, :, hb:] + b[:, hb:] + on_b.astype(F32),
                ],
                axis=1,
            ).astype(BF)
        )
    prefill_out = jnp.stack(finals)
    return (prefill_out, handed, decode_out)


def solution(mesh):
    placed = (
        P("seq", None, None),
        P(),
        P(),
        P(),
        P("head", None, "seq", None),
        P(),
        P(None, "head"),
        P(None, "head"),
        P(None, "head"),
        P("head", None),
        P(),
        P(),
    )
    return jax.shard_map(
        local,
        mesh=mesh,
        in_specs=placed,
        out_specs=(P("seq", None, "head"), P("head", None, "seq", None), P(None, None, "head")),
        check_vma=False,
    )
```

time: 230 us -> 103 us (0.45)
  waiting for transfers between devices: 72.6 us -> 10.9 us
  blocking collectives: 43.1 us -> 0 us
  Pallas kernels: 0 us -> 40.4 us
  matrix products: 40.1 us -> 0 us
  local copies, waits for them, and re-layouts: 37.5 us -> 18 us
  starting transfers between devices: 6.58 us -> 21.5 us
  between operations: 14.6 us -> 0.89 us
  other arithmetic: 13.5 us -> 10.6 us
    reduce_scatter x1 -> x0, waiting for transfers between devices: 53.2 us -> none  [local(): lax.psum_scatter(partial_out.astype(jnp.bfloat16), 'head', scatter_dimens...]
    all_gather x3 -> x0, blocking collectives: 43.1 us -> none  [combined_all(): pieces = jax.tree.map(lambda part: lax.all_gather(part, axis), value)]
    pallas_call x0 -> x7, Pallas kernels: none -> 40.4 us  [the longest x2 30.6 us: prefill(): pl.pallas_call(functools.partial(prefill_kernel, which, dec_rows, slots,...]
    dot_general x17 -> x0, matrix products: 40.1 us -> none  [the longest x1 9.54 us: local(): jnp.dot(attn, w_out, preferred_element_type=jnp.float32)]
    unnamed x3 -> x0, waiting for transfers between devices: 19.5 us -> none
    ppermute x0 -> x14, starting transfers between devices: none -> 17.7 us  [the longest x11 12.3 us: head_move(): return lax.ppermute(value, 'head', pairs)]
    dot_general x2 -> x0, local copies, waits for them, and re-layouts: 11.9 us -> none  [the longest x1 11.9 us: local(): jnp.dot(flat, w_query, preferred_element_type=jnp.float32)]
    ppermute x0 -> x14, waiting for transfers between devices: none -> 10.9 us  [the longest x11 10.2 us: head_move(): return lax.ppermute(value, 'head', pairs)]
  transfers between devices with their start and end apart: 3 -> 15, of which waited for: 2 -> 4; matrix products, arithmetic and copies ran while one was open for 25% -> 8% of each run, Pallas kernels for 0% -> 8%
where the time goes in v1:
time: 103 us; the launch traced here: 102 us
  Pallas kernels  40.4 us (39%)
  starting transfers between devices  21.5 us (21%)
  local copies, waits for them, and re-layouts  18 us (17%)
  waiting for transfers between devices  10.9 us (11%)
  other arithmetic  10.6 us (10%)
    pallas_call x2, Pallas kernels, prefill(): pl.pallas_call(functools.partial(prefill_kernel, which, dec_rows, slots,...  30.6 us
    unnamed x55, local copies, waits for them, and re-layouts  15.7 us
    ppermute x11, starting transfers between devices, head_move(): return lax.ppermute(value, 'head', pairs)  12.3 us
    ppermute x11, waiting for transfers between devices, head_move(): return lax.ppermute(value, 'head', pairs)  10.2 us
    ppermute x3, starting transfers between devices, local(): other = lax.ppermute(part, 'seq', [(i, i ^ bit) for i in range(n_seq)])  5.42 us
    convert_element_type x4, other arithmetic, local(): a, b = (a.astype(F32), b.astype(F32))  4.97 us
    all_to_all x1, starting transfers between devices, local(): lax.all_to_all(sending, 'seq', split_axis=1, concat_axis=0, tiled=True)  3.86 us
    pallas_call x1, Pallas kernels, own_parts(): pl.pallas_call(functools.partial(own_kernel, n_head), out_shape=[jax.Shap...  3.42 us
  transfers between devices with their start and end apart: 15, of which 4 were waited for; matrix products, arithmetic and copies ran while one was open for 8% of the time, Pallas kernels for 8%

profile of v1, /device:TPU:0, one launch (start us, length us, event | category | flops | bytes accessed | tf_op | source)
XLA Modules:
  0.0 102.3 jit_solution(12925191164687650399)
XLA Ops:
  0.6 0.9 reshape.89.refs_4_
  1.6 0.0 copy-start.1
  1.6 2.2 %copy-done.1 = bf16[2,256,4096]{2,1,0:T(8,128)(2,1)S(1)} copy-done((bf16[2,256,4096]{2,1,0:T(8,128)(2,1)S(1)}, bf16[2,256,4096]{2,1,0:T(8,128)(2,1)}, u32[]{:S(2)}) %copy-start.1) | copy-done | bytes 4194328
  3.8 1.2 %copy-done.2 = bf16[4096,128]{1,0:T(8,128)(2,1)S(1)} copy-done((bf16[4096,128]{1,0:T(8,128)(2,1)S(1)}, bf16[4096,128]{1,0:T(8,128)(2,1)}, u32[]{:S(2)}) %copy-start.2) | copy-done | bytes 1048600
  5.0 1.2 %copy-done.3 = bf16[4096,128]{1,0:T(8,128)(2,1)S(1)} copy-done((bf16[4096,128]{1,0:T(8,128)(2,1)S(1)}, bf16[4096,128]{1,0:T(8,128)(2,1)}, u32[]{:S(2)}) %copy-start.3) | copy-done | bytes 1048600
  6.2 0.9 copy-done.4
  7.2 0.7 copy-done.7
  7.8 0.7 copy-done.9
  8.5 0.7 copy-done.11
  9.1 0.7 copy-done.13
  9.8 0.7 copy-done.15
  10.4 0.7 copy-done.17
  11.1 0.0 copy-start.18
  11.1 14.8 %prefill_0.1 = (bf16[256,1024]{1,0:T(8,128)(2,1)S(1)}, bf16[256,1024]{1,0:T(8,128)(2,1)}, bf16[256,1024]{1,0:T(8,128)(2,1)S(1)}, bf16[256,256]{1,0:T(8,128)(2,1)S(1)}) custom-call(s32[16]{0:T(128)S(1)} %copy-done.11, s32[4]{0:T(128)S(1)} %copy-done.13, s32[4]{0:T(128)S(1)} %copy-done.15, bf16[2,256,4096]{2,1,0:T(8,128)(2,1)S(1)} %copy-done.1, ...), custom_call_target="tpu_custom_call" | custom-call | flops 3758096384 | bytes 18874368 | tf_op jit(solution)/shard_map/prefill_0/pallas_call | solution.py:202
  26.0 0.8 copy-done.20
  26.8 0.0 copy-start.19
  26.8 15.8 %prefill_1.1 = (bf16[256,1024]{1,0:T(8,128)(2,1)S(1)}, bf16[256,1024]{1,0:T(8,128)(2,1)}, bf16[256,1024]{1,0:T(8,128)(2,1)S(1)}, bf16[256,256]{1,0:T(8,128)(2,1)...) custom-call(s32[16]{0:T(128)S(1)} %copy-done.12, s32[4]{0:T(128)S(1)} %copy-done.14, s32[4]{0:T(128)S(1)} %copy-done.16, ...), custom_call_target="tpu_custom_call" | custom-call | flops 3925868544 | bytes 18874368 | tf_op jit(solution)/shard_map/prefill_1/pallas_call | solution.py:202
  42.6 1.7 %decode_attention.1 = (f32[136,128]{1,0:T(8,128)S(1)}, bf16[2,256,256]{2,1,0:T(8,128)(2,1)S(1)}) custom-call(s32[16]{0:T(128)S(1)} %copy-done.12, s32[4]{0:T(128)S(1)} %copy-done.14, s32[4]{0:T(128)S(1)} %copy-done.16, bf16[128,128]{1,0:T(8,128)(2,1)S(1)} %get-tuple-element.31.dq, bf16[16,256]{1,0:T(8,128)(2,1)S(1)} %get-tuple-element.32.dkv, ...), custom_call_target="tpu_custom_call" | custom-call | flops 419430400 | bytes 2097152 | tf_op jit(solution)/shard_map/decode_attention/pallas_call | solution.py:339
  44.4 0.0 copy-start.6
  44.4 0.5 collective-permute-start.8
  44.9 2.6 %collective-permute-start.6 = (bf16[256,1024]{1,0:T(8,128)(2,1)}, bf16[256,1024]{1,0:T(8,128)(2,1)}, u32[]{:S(2)}, u32[]{:S(2)}) collective-permute-start(bf16[256,1024]{1,0:T(8,128)(2,1)} %get-tuple-element.30), channel_id=1, source_target_pairs={{0,16},{8,24},{16,0},{24,8},{1,17},{9,25},{17,1},{25,9},{2,18},{10... | collective-permute-start | bytes 1572872 | tf_op jit(solution)/shard_map/ppermute | solution.py:449
  47.5 0.1 collective-permute-start.2
  47.6 0.6 copy-done.26
  48.2 1.7 %join_1.1.mine = f32[136,128]{1,0:T(8,128)} custom-call(f32[136,128]{1,0:T(8,128)} %copy-done.6, f32[136,128]{1,0:T(8,128)} %copy-done.26), custom_call_target="tpu_custom_call" | custom-call | tf_op jit(solution)/shard_map/join_1/pallas_call | solution.py:385
  49.9 2.0 %collective-permute-start.9 = (f32[136,128]{1,0:T(8,128)}, f32[136,128]{1,0:T(8,128)S(1)}, u32[]{:S(2)}, u32[]{:S(2)}) collective-permute-start(f32[136,128]{1,0:T(8,128)} %join_1.1.mine), channel_id=1, source_target_pairs={{0,2},{1,3},{2,0},{3,1},{4,6},{5,7},{6,4},{7,5},{8,10},{9,11},{10,... | collective-permute-start | bytes 208904 | tf_op jit(solution)/shard_map/ppermute | solution.py:464
  51.9 1.5 %collective-permute-start.4 = (bf16[256,1024]{1,0:T(8,128)(2,1)}, bf16[256,1024]{1,0:T(8,128)(2,1)}, u32[]{:S(2)}, u32[]{:S(2)}) collective-permute-start(bf16[256,1024]{1,0:T(8,128)(2,1)} %copy-done.21), channel_id=1, source_target_pairs={{0,8},{8,0},{16,24},{24,16},{1,9},{9,1},{17,25},{25,17},{2,10},{10... | collective-permute-start | bytes 1572872 | tf_op jit(solution)/shard_map/ppermute | solution.py:449
  53.4 0.5 collective-permute-start
  53.9 0.7 copy.18
  54.6 3.9 %all-to-all-start = ((bf16[2,8,32,256]{3,2,0,1:T(8,128)(2,1)}), bf16[2,8,32,256]{3,2,0,1:T(8,128)(2,1)S(1)}, u32[]{:S(2)}, u32[]{:S(2)}) async-start(bf16[2,8,32,256]{3,2,0,1:T(8,128)(2,1)} %copy.18), calls=%async_computation | async-start | bytes 524288 | tf_op jit(solution)/shard_map/all_to_all | solution.py:477
  58.5 0.0 collective-permute-done.9.other
  58.5 0.0 copy-start.25
  58.5 0.6 copy-done.25
  59.1 1.7 %join_2.1.mine = f32[136,128]{1,0:T(8,128)} custom-call(f32[136,128]{1,0:T(8,128)} %join_1.1.mine, f32[136,128]{1,0:T(8,128)} %copy-done.25), custom_call_target="tpu_custom_call" | custom-call | tf_op jit(solution)/shard_map/join_2/pallas_call | solution.py:385
  60.8 2.9 %collective-permute-start.10 = (f32[136,128]{1,0:T(8,128)}, f32[136,128]{1,0:T(8,128)S(1)}, u32[]{:S(2)}, u32[]{:S(2)}) collective-permute-start(f32[136,128]{1,0:T(8,128)} %join_2.1.mine), channel_id=1, source_target_pairs={{0,4},{1,5},{2,6},{3,7},{4,0},{5,1},{6,2},{7,3},{8,12},{9,13},{10,... | collective-permute-start | bytes 208904 | tf_op jit(solution)/shard_map/ppermute | solution.py:464
  63.7 3.4 %copy-done = bf16[1024,4096]{1,0:T(8,128)(2,1)S(1)} copy-done((bf16[1024,4096]{1,0:T(8,128)(2,1)S(1)}, bf16[1024,4096]{1,0:T(8,128)(2,1)}, u32[]{:S(2)}) %copy-start) | copy-done | bytes 8388632
  67.1 3.4 %own_parts.1 = (f32[2,256,512]{2,1,0:T(8,128)S(1)}, f32[2,256,512]{2,1,0:T(8,128)S(1)}, f32[2,256,1024]{2,1,0:T(8,128)S(1)}) custom-call(bf16[256,1024]{1,0:T(8,128)(2,1)S(1)} %get-tuple-element.22.attn0, bf16[256,1024]{1,0:T(8,128)(2,1)S(1)} %get-tuple-element.23.attn1, bf16[1024,4096]{1,0:T(8,128)(2,1)S(1)} %copy-done), custom_call_target="tpu_custom_call" | custom-call | flops 2147483648 | bytes 9437184 | tf_op jit(solution)/shard_map/own_parts/pallas_call | solution.py:258
  70.5 0.7 collective-permute-done.10.other
  71.2 1.3 %decode_project.1 = (bf16[16,1024]{1,0:T(8,128)(2,1)S(1)}, bf16[16,1024]{1,0:T(8,128)(2,1)S(1)}, bf16[16,1024]{1,0:T(8,128)(2,1)S(1)}, bf16[16,1024]{1,0:T(8,128)(2,1)S(1)}) custom-call(f32[136,128]{1,0:T(8,128)S(1)} %copy-done.5, f32[136,128]{1,0:T(8,128)S(1)} %collective-permute-done.10.other, bf16[1024,4096]{1,0:T(8,128)(2,1)S(1)} %copy-done), custom_call_target="tpu_custom_call" | custom-call | flops 2147483648 | bytes 8388608 | tf_op jit(solution)/shard_map/decode_project/pallas_call | solution.py:415
  72.5 1.5 %collective-permute-start.11 = (bf16[16,1024]{1,0:T(8,128)(2,1)S(1)}, bf16[16,1024]{1,0:T(8,128)(2,1)S(1)}, u32[]{:S(2)}, u32[]{:S(2)}) collective-permute-start(bf16[16,1024]{1,0:T(8,128)(2,1)S(1)} %get-tuple-element.38), channel_id=1, source_target_pairs={{0,8},{8,0},{16,24},{24,16},{1,9},{9,1},{17,25},{25,17},{2,10},{10... | collective-permute-start | bytes 98312 | tf_op jit(solution)/shard_map/ppermute | solution.py:449
  74.0 1.5 %collective-permute-start.12 = (bf16[16,1024]{1,0:T(8,128)(2,1)S(1)}, bf16[16,1024]{1,0:T(8,128)(2,1)S(1)}, u32[]{:S(2)}, u32[]{:S(2)}) collective-permute-start(bf16[16,1024]{1,0:T(8,128)(2,1)S(1)} %get-tuple-element.39), channel_id=1, source_target_pairs={{0,16},{8,24},{16,0},{24,8},{1,17},{9,25},{17,1},{25,9},{2,18},{10... | collective-permute-start | bytes 98312 | tf_op jit(solution)/shard_map/ppermute | solution.py:449
  75.5 1.1 %convert_element_type.76 = f32[256,1024]{1,0:T(8,128)S(1)} convert(bf16[256,1024]{1,0:T(8,128)(2,1)} %collective-permute-done.6) | non-fusion elementwise | flops 262144 | bytes 1572864 | tf_op jit(solution)/shard_map/convert_element_type | solution.py:483
  76.7 1.1 %convert_element_type.70 = f32[256,1024]{1,0:T(8,128)S(1)} convert(bf16[256,1024]{1,0:T(8,128)(2,1)} %collective-permute-done.2) | non-fusion elementwise | flops 262144 | bytes 1572864 | tf_op jit(solution)/shard_map/convert_element_type | solution.py:483
  77.9 1.1 %fusion.6 = (bf16[256,512]{1,0:T(8,128)(2,1)}, bf16[256,512]{1,0:T(8,128)(2,1)}) fusion(f32[256,1024]{1,0:T(8,128)S(1)} %convert_element_type.70, f32[2,256,512]{2,1,0:T(8,128)S(1)} %get-tuple-element.28, f32[256,1024]{1,0:T(8,128)S(1)} %convert_element_type.76), kind=kLoop, calls=%fused_computation.12 | loop fusion | flops 524288 | bytes 2621440 | tf_op jit(solution)/shard_map/convert_element_type | solution.py:485
  79.0 0.5 collective-permute-start.3
  79.5 0.0 collective-permute-done.4
  79.5 1.5 %collective-permute-start.7 = (bf16[256,512]{1,0:T(8,128)(2,1)}, bf16[256,512]{1,0:T(8,128)(2,1)}, u32[]{:S(2)}, u32[]{:S(2)}) collective-permute-start(bf16[256,512]{1,0:T(8,128)(2,1)} %get-tuple-element.48), channel_id=1, source_target_pairs={{0,8},{8,0},{16,24},{24,16},{1,9},{9,1},{17,25},{25,17},{2,10},{10... | collective-permute-start | bytes 786440 | tf_op jit(solution)/shard_map/ppermute | solution.py:449
  81.0 1.1 %convert_element_type.73 = f32[256,1024]{1,0:T(8,128)S(1)} convert(bf16[256,1024]{1,0:T(8,128)(2,1)} %collective-permute-done.4) | non-fusion elementwise | flops 262144 | bytes 1572864 | tf_op jit(solution)/shard_map/convert_element_type | solution.py:483
  82.2 1.5 %convert_element_type.67 = f32[256,1024]{1,0:T(8,128)S(1)} convert(bf16[256,1024]{1,0:T(8,128)(2,1)} %collective-permute-done) | non-fusion elementwise | flops 262144 | bytes 1572864 | tf_op jit(solution)/shard_map/convert_element_type | solution.py:483
  83.7 0.0 copy-start.24
  83.7 1.1 %fusion.9 = (bf16[256,512]{1,0:T(8,128)(2,1)}, bf16[256,512]{1,0:T(8,128)(2,1)}) fusion(f32[256,1024]{1,0:T(8,128)S(1)} %convert_element_type.67, f32[2,256,512]{2,1,0:T(8,128)S(1)} %get-tuple-element.26, f32[256,1024]{1,0:T(8,128)S(1)} %convert_element_type.73), kind=kLoop, calls=%fused_computation.17 | loop fusion | flops 524288 | bytes 2621440 | tf_op jit(solution)/shard_map/convert_element_type | solution.py:484
  84.8 0.5 collective-permute-start.1
  85.4 0.0 collective-permute-done.11
  85.4 1.5 %collective-permute-start.5 = (bf16[256,512]{1,0:T(8,128)(2,1)}, bf16[256,512]{1,0:T(8,128)(2,1)}, u32[]{:S(2)}, u32[]{:S(2)}) collective-permute-start(bf16[256,512]{1,0:T(8,128)(2,1)} %get-tuple-element.46), channel_id=1, source_target_pairs={{0,16},{8,24},{16,0},{24,8},{1,17},{9,25},{17,1},{25,9},{2,18},{10... | collective-permute-start | bytes 786440 | tf_op jit(solution)/shard_map/ppermute | solution.py:449
  86.9 0.5 collective-permute-start.13
  87.4 5.5 %collective-permute-done.13 = bf16[16,1024]{1,0:T(8,128)(2,1)S(1)} collective-permute-done((bf16[16,1024]{1,0:T(8,128)(2,1)S(1)}, bf16[16,1024]{1,0:T(8,128)(2,1)S(1)}, u32[]{:S(2)}, u32[]{:S(2)}) %collective-permute-start.13) | collective-permute-done | bytes 32800 | tf_op jit(solution)/shard_map/ppermute | solution.py:449
  92.9 0.6 reshape.92
  93.5 0.0 all-to-all-done
  93.5 0.0 collective-permute-done.3
  93.5 0.0 collective-permute-done.7
  93.5 1.6 %collective-permute-done.1 = bf16[256,512]{1,0:T(8,128)(2,1)} collective-permute-done((bf16[256,512]{1,0:T(8,128)(2,1)}, bf16[256,512]{1,0:T(8,128)(2,1)}, u32[]{:S(2)}, u32[]{:S(2)}) %collective-permute-start.1) | collective-permute-done | bytes 262176 | tf_op jit(solution)/shard_map/ppermute | solution.py:449
  95.1 3.1 %collective-permute-done.5 = bf16[256,512]{1,0:T(8,128)(2,1)} collective-permute-done((bf16[256,512]{1,0:T(8,128)(2,1)}, bf16[256,512]{1,0:T(8,128)(2,1)}, u32[]{:S(2)}, u32[]{:S(2)}) %collective-permute-start.5) | collective-permute-done | bytes 262176 | tf_op jit(solution)/shard_map/ppermute | solution.py:449
  98.2 2.3 %fusion.12 = (bf16[1,256,512]{2,1,0:T(8,128)(2,1)S(1)}, bf16[1,256,512]{2,1,0:T(8,128)(2,1)S(1)}, bf16[1,256,512]{2,1,0:T(8,128)(2,1)S(1)}, bf16[1,256,512]{2,1,0:T(8,128)(2,1)S(1)}) fusion(bf16[256,512]{1,0:T(8,128)(2,1)} %collective-permute-done.1, f32[256,1024]{1,0:T(8,128)} %copy-done.24, f32[2,256,1024]{2,1,0:T(8,128)S(1)} %get-tuple-element.24, ...), kind=kLoop, calls=%fused_computation.21 | loop fusion | flops 2097152 | bytes 6291456 | tf_op jit(solution)/shard_map/concatenate | solution.py:487
  100.5 1.1 %maximum_maximum_fusion = bf16[2,256,1024]{2,1,0:T(8,128)(2,1)} fusion(bf16[1,256,512]{2,1,0:T(8,128)(2,1)S(1)} %get-tuple-element.42, bf16[1,256,512]{2,1,0:T(8,128)(2,1)S(1)} %get-tuple-element.43, bf16[1,256,512]{2,1,0:T(8,128)(2,1)S(1)} %get-tuple-element.44, bf16[1,256,512]{2,1,0:T(8,128)(2,1)S(1)} %get-tuple-element.41), kind=kLoop, calls=%fused_computation | loop fusion | flops 4194304 | bytes 2097152 | tf_op jit(solution)/shard_map/stack | solution.py:495
  101.6 0.7 copy.20
  (40 shorter events, 0.1 us)
Async XLA Ops:
  1.6 2.2 %copy-start.1 = (bf16[2,256,4096]{2,1,0:T(8,128)(2,1)S(1)}, bf16[2,256,4096]{2,1,0:T(8,128)(2,1)}, u32[]{:S(2)}) copy-start(bf16[2,256,4096]{2,1,0:T(8,128)(2,1)} %refs_3_.3) | copy-start | bytes 12582916
  3.8 1.2 %copy-start.2 = (bf16[4096,128]{1,0:T(8,128)(2,1)S(1)}, bf16[4096,128]{1,0:T(8,128)(2,1)}, u32[]{:S(2)}) copy-start(bf16[4096,128]{1,0:T(8,128)(2,1)} %refs_6_.3) | copy-start | bytes 3145732
  5.0 1.2 %copy-start.3 = (bf16[4096,128]{1,0:T(8,128)(2,1)S(1)}, bf16[4096,128]{1,0:T(8,128)(2,1)}, u32[]{:S(2)}) copy-start(bf16[4096,128]{1,0:T(8,128)(2,1)} %refs_7_.3) | copy-start | bytes 3145732
  6.2 0.9 copy-start.4
  7.2 0.7 copy-start.7
  7.8 0.7 copy-start.9
  8.5 0.7 copy-start.11
  9.1 0.7 copy-start.13
  9.8 0.7 copy-start.15
  10.4 0.7 copy-start.17
  11.1 15.7 %copy-start.8 = (f32[128]{0:T(128)S(1)}, f32[128]{0:T(128)}, u32[]{:S(2)}) copy-start(f32[128]{0:T(128)} %param.24) | copy-start | bytes 1540
  11.1 15.7 %copy-start.10 = (f32[128]{0:T(128)S(1)}, f32[128]{0:T(128)}, u32[]{:S(2)}) copy-start(f32[128]{0:T(128)} %param.25) | copy-start | bytes 1540
  11.1 15.7 %copy-start.12 = (s32[16]{0:T(128)S(1)}, s32[16]{0:T(128)}, u32[]{:S(2)}) copy-start(s32[16]{0:T(128)} %plen.1) | copy-start | bytes 196
  11.1 15.7 %copy-start.14 = (s32[4]{0:T(128)S(1)}, s32[4]{0:T(128)}, u32[]{:S(2)}) copy-start(s32[4]{0:T(128)} %adm.1) | copy-start | bytes 52
  11.1 15.7 %copy-start.16 = (s32[4]{0:T(128)S(1)}, s32[4]{0:T(128)}, u32[]{:S(2)}) copy-start(s32[4]{0:T(128)} %clen.1) | copy-start | bytes 52
  11.1 15.7 %copy-start.18 = (f32[1,128]{1,0:T(1,128)S(1)}, f32[1,128]{1,0:T(1,128)}, u32[]{:S(2)}) copy-start(f32[1,128]{1,0:T(1,128)} %constant.5.clone.refs_11_.refs_12_) | copy-start | bytes 1540
  26.0 0.8 copy-start.20
  26.8 15.8 %copy-start.19 = (bf16[1,4,512,256]{3,2,1,0:T(8,128)(2,1)S(1)}, bf16[1,4,512,256]{3,2,1,0:T(8,128)(2,1)}, u32[]{:S(2)}) copy-start(bf16[1,4,512,256]{3,2,1,0:T(8,128)(2,1)} %param.18) | copy-start | bytes 3145732
  42.6 1.8 %copy-start.21 = (bf16[256,1024]{1,0:T(8,128)(2,1)}, bf16[256,1024]{1,0:T(8,128)(2,1)S(1)}, u32[]{:S(2)}) copy-start(bf16[256,1024]{1,0:T(8,128)(2,1)S(1)} %get-tuple-element.29) | copy-start | bytes 1572868
  44.4 3.2 %copy-start.6 = (f32[136,128]{1,0:T(8,128)}, f32[136,128]{1,0:T(8,128)S(1)}, u32[]{:S(2)}) copy-start(f32[136,128]{1,0:T(8,128)S(1)} %get-tuple-element.36.mine) | copy-start | bytes 208900
  44.4 3.2 %collective-permute-start.8 = (f32[136,128]{1,0:T(8,128)S(1)}, f32[136,128]{1,0:T(8,128)S(1)}, u32[]{:S(2)}, u32[]{:S(2)}) collective-permute-start(f32[136,128]{1,0:T(8,128)S(1)} %get-tuple-element.36.mine), channel_id=1, source_target_pairs={{0,1},{1,0},{2,3},{3,2},{4,5},{5,4},{6,7},{7,6},{8,9},{9,8},{10,11... | collective-permute-start | bytes 208904 | tf_op jit(solution)/shard_map/ppermute | solution.py:464
  44.9 29.1 %collective-permute-start.6 = (bf16[256,1024]{1,0:T(8,128)(2,1)}, bf16[256,1024]{1,0:T(8,128)(2,1)}, u32[]{:S(2)}, u32[]{:S(2)}) collective-permute-start(bf16[256,1024]{1,0:T(8,128)(2,1)} %get-tuple-element.30), channel_id=1, source_target_pairs={{0,16},{8,24},{16,0},{24,8},{1,17},{9,25},{17,1},{25,9},{2,18},{10... | collective-permute-start | bytes 1572872 | tf_op jit(solution)/shard_map/ppermute | solution.py:449
  47.5 29.2 %collective-permute-start.2 = (bf16[256,1024]{1,0:T(8,128)(2,1)}, bf16[256,1024]{1,0:T(8,128)(2,1)}, u32[]{:S(2)}, u32[]{:S(2)}) collective-permute-start(bf16[256,1024]{1,0:T(8,128)(2,1)} %get-tuple-element.27), channel_id=1, source_target_pairs={{0,16},{8,24},{16,0},{24,8},{1,17},{9,25},{17,1},{25,9},{2,18},{10... | collective-permute-start | bytes 1572872 | tf_op jit(solution)/shard_map/ppermute | solution.py:449
  47.6 0.6 copy-start.26
  49.9 8.6 %collective-permute-start.9 = (f32[136,128]{1,0:T(8,128)}, f32[136,128]{1,0:T(8,128)S(1)}, u32[]{:S(2)}, u32[]{:S(2)}) collective-permute-start(f32[136,128]{1,0:T(8,128)} %join_1.1.mine), channel_id=1, source_target_pairs={{0,2},{1,3},{2,0},{3,1},{4,6},{5,7},{6,4},{7,5},{8,10},{9,11},{10,... | collective-permute-start | bytes 208904 | tf_op jit(solution)/shard_map/ppermute | solution.py:464
  51.9 27.6 %collective-permute-start.4 = (bf16[256,1024]{1,0:T(8,128)(2,1)}, bf16[256,1024]{1,0:T(8,128)(2,1)}, u32[]{:S(2)}, u32[]{:S(2)}) collective-permute-start(bf16[256,1024]{1,0:T(8,128)(2,1)} %copy-done.21), channel_id=1, source_target_pairs={{0,8},{8,0},{16,24},{24,16},{1,9},{9,1},{17,25},{25,17},{2,10},{10... | collective-permute-start | bytes 1572872 | tf_op jit(solution)/shard_map/ppermute | solution.py:449
  53.4 28.8 %collective-permute-start = (bf16[256,1024]{1,0:T(8,128)(2,1)}, bf16[256,1024]{1,0:T(8,128)(2,1)}, u32[]{:S(2)}, u32[]{:S(2)}) collective-permute-start(bf16[256,1024]{1,0:T(8,128)(2,1)} %copy-done.20), channel_id=1, source_target_pairs={{0,8},{8,0},{16,24},{24,16},{1,9},{9,1},{17,25},{25,17},{2,10},{10... | collective-permute-start | bytes 1572872 | tf_op jit(solution)/shard_map/ppermute | solution.py:449
  54.6 38.9 %all-to-all-start = ((bf16[2,8,32,256]{3,2,0,1:T(8,128)(2,1)}), bf16[2,8,32,256]{3,2,0,1:T(8,128)(2,1)S(1)}, u32[]{:S(2)}, u32[]{:S(2)}) async-start(bf16[2,8,32,256]{3,2,0,1:T(8,128)(2,1)} %copy.18), calls=%async_computation | async-start | bytes 524288 | tf_op jit(solution)/shard_map/all_to_all | solution.py:477
  58.5 0.6 copy-start.25
  60.8 10.4 %collective-permute-start.10 = (f32[136,128]{1,0:T(8,128)}, f32[136,128]{1,0:T(8,128)S(1)}, u32[]{:S(2)}, u32[]{:S(2)}) collective-permute-start(f32[136,128]{1,0:T(8,128)} %join_2.1.mine), channel_id=1, source_target_pairs={{0,4},{1,5},{2,6},{3,7},{4,0},{5,1},{6,2},{7,3},{8,12},{9,13},{10,... | collective-permute-start | bytes 208904 | tf_op jit(solution)/shard_map/ppermute | solution.py:464
  63.7 3.4 %copy-start = (bf16[1024,4096]{1,0:T(8,128)(2,1)S(1)}, bf16[1024,4096]{1,0:T(8,128)(2,1)}, u32[]{:S(2)}) copy-start(bf16[1024,4096]{1,0:T(8,128)(2,1)} %wo.1) | copy-start | bytes 25165828
  67.1 4.1 %copy-start.5 = (f32[136,128]{1,0:T(8,128)S(1)}, f32[136,128]{1,0:T(8,128)}, u32[]{:S(2)}) copy-start(f32[136,128]{1,0:T(8,128)} %join_2.1.mine) | copy-start | bytes 208900
  72.5 12.9 %collective-permute-start.11 = (bf16[16,1024]{1,0:T(8,128)(2,1)S(1)}, bf16[16,1024]{1,0:T(8,128)(2,1)S(1)}, u32[]{:S(2)}, u32[]{:S(2)}) collective-permute-start(bf16[16,1024]{1,0:T(8,128)(2,1)S(1)} %get-tuple-element.38), channel_id=1, source_target_pairs={{0,8},{8,0},{16,24},{24,16},{1,9},{9,1},{17,25},{25,17},{2,10},{10... | collective-permute-start | bytes 98312 | tf_op jit(solution)/shard_map/ppermute | solution.py:449
  74.0 12.9 %collective-permute-start.12 = (bf16[16,1024]{1,0:T(8,128)(2,1)S(1)}, bf16[16,1024]{1,0:T(8,128)(2,1)S(1)}, u32[]{:S(2)}, u32[]{:S(2)}) collective-permute-start(bf16[16,1024]{1,0:T(8,128)(2,1)S(1)} %get-tuple-element.39), channel_id=1, source_target_pairs={{0,16},{8,24},{16,0},{24,8},{1,17},{9,25},{17,1},{25,9},{2,18},{10... | collective-permute-start | bytes 98312 | tf_op jit(solution)/shard_map/ppermute | solution.py:449
  77.8 4.3 %copy-start.22 = (f32[256,1024]{1,0:T(8,128)}, f32[256,1024]{1,0:T(8,128)S(1)}, u32[]{:S(2)}) copy-start(f32[256,1024]{1,0:T(8,128)S(1)} %convert_element_type.70) | copy-start | bytes 3145732
  79.0 14.5 %collective-permute-start.3 = (bf16[256,512]{1,0:T(8,128)(2,1)}, bf16[256,512]{1,0:T(8,128)(2,1)}, u32[]{:S(2)}, u32[]{:S(2)}) collective-permute-start(bf16[256,512]{1,0:T(8,128)(2,1)} %get-tuple-element.47), channel_id=1, source_target_pairs={{0,8},{8,0},{16,24},{24,16},{1,9},{9,1},{17,25},{25,17},{2,10},{10... | collective-permute-start | bytes 786440 | tf_op jit(solution)/shard_map/ppermute | solution.py:449
  79.5 14.0 %collective-permute-start.7 = (bf16[256,512]{1,0:T(8,128)(2,1)}, bf16[256,512]{1,0:T(8,128)(2,1)}, u32[]{:S(2)}, u32[]{:S(2)}) collective-permute-start(bf16[256,512]{1,0:T(8,128)(2,1)} %get-tuple-element.48), channel_id=1, source_target_pairs={{0,8},{8,0},{16,24},{24,16},{1,9},{9,1},{17,25},{25,17},{2,10},{10... | collective-permute-start | bytes 786440 | tf_op jit(solution)/shard_map/ppermute | solution.py:449
  82.2 2.7 %copy-start.23 = (f32[256,1024]{1,0:T(8,128)}, f32[256,1024]{1,0:T(8,128)S(1)}, u32[]{:S(2)}) copy-start(f32[256,1024]{1,0:T(8,128)S(1)} %convert_element_type.73) | copy-start | bytes 3145732
  83.7 9.1 %copy-start.24 = (f32[256,1024]{1,0:T(8,128)}, f32[256,1024]{1,0:T(8,128)S(1)}, u32[]{:S(2)}) copy-start(f32[256,1024]{1,0:T(8,128)S(1)} %convert_element_type.67) | copy-start | bytes 3145732
  84.8 10.3 %collective-permute-start.1 = (bf16[256,512]{1,0:T(8,128)(2,1)}, bf16[256,512]{1,0:T(8,128)(2,1)}, u32[]{:S(2)}, u32[]{:S(2)}) collective-permute-start(bf16[256,512]{1,0:T(8,128)(2,1)} %get-tuple-element.45), channel_id=1, source_target_pairs={{0,16},{8,24},{16,0},{24,8},{1,17},{9,25},{17,1},{25,9},{2,18},{10... | collective-permute-start | bytes 786440 | tf_op jit(solution)/shard_map/ppermute | solution.py:449
  85.4 12.9 %collective-permute-start.5 = (bf16[256,512]{1,0:T(8,128)(2,1)}, bf16[256,512]{1,0:T(8,128)(2,1)}, u32[]{:S(2)}, u32[]{:S(2)}) collective-permute-start(bf16[256,512]{1,0:T(8,128)(2,1)} %get-tuple-element.46), channel_id=1, source_target_pairs={{0,16},{8,24},{16,0},{24,8},{1,17},{9,25},{17,1},{25,9},{2,18},{10... | collective-permute-start | bytes 786440 | tf_op jit(solution)/shard_map/ppermute | solution.py:449
  86.9 5.9 %collective-permute-start.13 = (bf16[16,1024]{1,0:T(8,128)(2,1)S(1)}, bf16[16,1024]{1,0:T(8,128)(2,1)S(1)}, u32[]{:S(2)}, u32[]{:S(2)}) collective-permute-start(bf16[16,1024]{1,0:T(8,128)(2,1)S(1)} %get-tuple-element.40), channel_id=1, source_target_pairs={{0,24},{8,16},{16,8},{24,0},{1,25},{9,17},{17,9},{25,1},{2,26},{10... | collective-permute-start | bytes 98312 | tf_op jit(solution)/shard_map/ppermute | solution.py:449

commit v2 on v1

v2 whole, which is shorter than its diff:
```python
import functools

import jax
import jax.numpy as jnp
import numpy as np
from jax import lax
from jax.experimental import pallas as pl
from jax.experimental.pallas import tpu as pltpu
from jax.sharding import PartitionSpec as P

HD = 128
EPS = 1e-06
THETA = 1000000.0
NEG = -1e30
LOG2E = 1.4426950408889634
SCALE = HD**-0.5
C2 = SCALE * LOG2E
BF = jnp.bfloat16
F32 = jnp.float32
HB = pl.BlockSpec(memory_space=pltpu.HBM)
BRIEF = pl.CostEstimate(flops=1, bytes_accessed=1, transcendentals=0)
VM = pl.BlockSpec(memory_space=pltpu.VMEM)
SM = pl.BlockSpec(memory_space=pltpu.SMEM)
MIB = 1024 * 1024


def frequencies():
    half = HD // 2
    freq = np.float32(THETA) ** (-np.arange(half, dtype=np.float32) / np.float32(half))
    return freq.astype(np.float32)


def prompt_table(length):
    angle = np.arange(length, dtype=np.float32)[:, None] * frequencies()[None, :]
    cosine, sine = np.cos(angle), np.sin(angle)
    return np.concatenate([cosine, cosine, -sine, sine], axis=1).astype(np.float32)


def dot(a, b):
    return jnp.dot(a, b, preferred_element_type=F32)


def dot_nt(a, b):
    return lax.dot_general(a, b, (((1,), (1,)), ((), ())), preferred_element_type=F32)


def norm(values, gain):
    square = jnp.mean(values * values, axis=-1, keepdims=True)
    return values * lax.rsqrt(square + EPS) * gain


def rope(values, cos2, sin2):
    return values * cos2 + pltpu.roll(values, HD // 2, 1) * sin2


def effective_lengths(plen, adm, clen, slots):
    out = []
    for r in range(slots):
        taken = adm[r]
        out.append(jnp.where(taken >= 0, plen[jnp.maximum(taken, 0)], clen[r]))
    return out


def by_slot(index, values):
    result = jnp.full(index.shape, values[0])
    for r in range(1, len(values)):
        result = jnp.where(index == r, values[r], result)
    return result


def prefill_kernel(which, dec_rows, slots, n_head, *refs):
    it = iter(refs)
    plen_h, adm_h, clen_h = next(it), next(it), next(it)
    x_hbm = next(it)
    dec_hbm = next(it) if dec_rows else None
    wq_hbm, wk_hbm, wv_hbm, wo_hbm = next(it), next(it), next(it), next(it)
    smalls_h = [next(it) for _ in range(4)]
    send_a, send_b, attn, kv_out = next(it), next(it), next(it), next(it)
    if dec_rows:
        dq_out, dkv_out = next(it), next(it)
    x_v, wkv_v, wq_v, wo_v, acc = next(it), next(it), next(it), next(it), next(it)
    plen, adm, clen = next(it), next(it), next(it)
    qg, kg, table, freq = next(it), next(it), next(it), next(it)
    x_sem, dec_sem, wkv_sem, wq_sem, wo_sem, small_sem = it

    rows, width = kv_out.shape[0], x_hbm.shape[2]
    chunks, _, depth = x_v.shape
    local = wq_v.shape[1]
    nb = width // n_head
    hb = nb // 2
    head = lax.axis_index("head")
    flip_x = head + 1 - 2 * lax.rem(head, 2)
    flip_y = lax.rem(head + 2, 4)
    flip_xy = 3 - head

    steps = []
    for c in range(chunks):
        at = pl.ds(c * depth, depth)
        group = [
            pltpu.make_async_copy(
                x_hbm.at[which, :, at], x_v.at[c, pl.ds(0, rows)], x_sem.at[c]
            ),
            pltpu.make_async_copy(wk_hbm.at[at], wkv_v.at[at, pl.ds(0, HD)], wkv_sem.at[0, c]),
            pltpu.make_async_copy(wv_hbm.at[at], wkv_v.at[at, pl.ds(HD, HD)], wkv_sem.at[1, c]),
            pltpu.make_async_copy(wq_hbm.at[at], wq_v.at[at], wq_sem.at[c]),
        ]
        if dec_rows:
            group.append(
                pltpu.make_async_copy(
                    dec_hbm.at[:, at], x_v.at[c, pl.ds(rows, dec_rows)], dec_sem.at[c]
                )
            )
        steps.append(group)
    small = [
        pltpu.make_async_copy(src, dst, small_sem.at[i])
        for i, (src, dst) in enumerate(
            zip([plen_h, adm_h, clen_h] + smalls_h, [plen, adm, clen, qg, kg, table, freq])
        )
    ]
    places = [(flip_xy * nb, 0, nb), (flip_x * nb, nb, hb), (flip_y * nb + hb, nb + hb, hb)]
    o_copies = [
        pltpu.make_async_copy(
            wo_hbm.at[:, pl.ds(pl.multiple_of(src, hb), size)],
            wo_v.at[:, pl.ds(dst, size)],
            wo_sem.at[j],
        )
        for j, (src, dst, size) in enumerate(places)
    ]
    queue = steps + [[copy] for copy in o_copies]
    ahead = 4
    for copy in queue[0]:
        copy.start()
    for copy in small:
        copy.start()
    for group in queue[1:ahead]:
        for copy in group:
            copy.start()

    for c in range(chunks):
        for copy in steps[c]:
            copy.wait()
        if c + ahead < len(queue):
            for copy in queue[c + ahead]:
                copy.start()
        at = slice(c * depth, (c + 1) * depth)
        block = x_v[c]
        kv_part = dot(block, wkv_v[at, :])
        q_part = dot(block, wq_v[at, :])
        if c == 0:
            acc[:, local:] = kv_part
            acc[:, :local] = q_part
        else:
            acc[:, local:] += kv_part
            acc[:, :local] += q_part

    for copy in small:
        copy.wait()
    length = plen[lax.axis_index("seq") * x_hbm.shape[0] + which]
    row_at = lax.broadcasted_iota(jnp.int32, (rows, rows), 0)
    col_at = lax.broadcasted_iota(jnp.int32, (rows, rows), 1)
    bias = jnp.where((col_at <= row_at) & (col_at < length), 0.0, NEG).astype(F32)
    cos2, sin2 = table[:, :HD], table[:, HD:]
    key = rope(norm(acc[:rows, local : local + HD], kg[...]), cos2, sin2).astype(BF)
    value = acc[:rows, local + HD :].astype(BF)
    kv_out[:, :HD] = key
    kv_out[:, HD:] = value
    if dec_rows:
        eff = effective_lengths(plen, adm, clen, slots)
        row = lax.broadcasted_iota(jnp.int32, (dec_rows, HD), 0)
        spots = by_slot(lax.rem(row, slots), eff) + row // slots
        angle = spots.astype(F32) * freq[...]
        lane = lax.broadcasted_iota(jnp.int32, (dec_rows, HD), 1)
        dcos2 = jnp.cos(angle)
        dsin2 = jnp.where(lane < HD // 2, -1.0, 1.0) * jnp.sin(angle)
        dkv_out[:, :HD] = rope(norm(acc[rows:, local : local + HD], kg[...]), dcos2, dsin2).astype(BF)
        dkv_out[:, HD:] = acc[rows:, local + HD :].astype(BF)

    for h in range(local // HD):
        at = slice(h * HD, (h + 1) * HD)
        query = rope(norm(acc[:rows, at], qg[...]), cos2, sin2).astype(BF)
        if dec_rows:
            dq_out[h * dec_rows : (h + 1) * dec_rows, :] = rope(
                norm(acc[rows:, at], qg[...]), dcos2, dsin2
            ).astype(BF)
        scores = dot_nt(query, key) + bias
        top = jnp.max(scores, axis=-1, keepdims=True)
        expo = jnp.exp2((scores - top) * C2)
        total = jnp.sum(expo, axis=-1, keepdims=True)
        weights = (expo * (1.0 / total)).astype(BF)
        attn[:, at] = dot(weights, value).astype(BF)

    for copy in o_copies:
        copy.wait()
    mixed = attn[...]
    diag = dot(mixed, wo_v[:, :nb]).astype(BF)
    send_a[:, :hb] = diag[:, :hb]
    send_b[:, :hb] = diag[:, hb:]
    rest = dot(mixed, wo_v[:, nb:]).astype(BF)
    send_a[:, hb:] = rest[:, :hb]
    send_b[:, hb:] = rest[:, hb:]


def prefill(which, with_dec, n_head, plen, adm, clen, x, dec, wq, wk, wv, wo, qg, kg, table, freq):
    _, rows, width = x.shape
    slots = adm.shape[0]
    dec_rows = dec.shape[0] if with_dec else 0
    local = wq.shape[1]
    chunks = 8
    nb = width // n_head
    hb = nb // 2
    outs = [
        jax.ShapeDtypeStruct((rows, nb), BF),
        jax.ShapeDtypeStruct((rows, nb), BF),
        jax.ShapeDtypeStruct((rows, local), BF),
        jax.ShapeDtypeStruct((rows, 2 * HD), BF),
    ]
    if with_dec:
        outs += [
            jax.ShapeDtypeStruct((dec_rows * (local // HD), HD), BF),
            jax.ShapeDtypeStruct((dec_rows, 2 * HD), BF),
        ]
    args = [plen, adm, clen, x] + ([dec] if with_dec else []) + [wq, wk, wv, wo, qg, kg, table, freq]
    total_rows = rows + dec_rows
    return pl.pallas_call(
        functools.partial(prefill_kernel, which, dec_rows, slots, n_head),
        out_shape=outs,
        in_specs=[HB] * len(args),
        out_specs=[VM] * len(outs),
        scratch_shapes=[
            pltpu.VMEM((chunks, total_rows, width // chunks), BF),
            pltpu.VMEM((width, 2 * HD), BF),
            pltpu.VMEM((width, local), BF),
            pltpu.VMEM((local, 2 * nb), BF),
            pltpu.VMEM((total_rows, local + 2 * HD), F32),
            pltpu.SMEM(plen.shape, jnp.int32),
            pltpu.SMEM(adm.shape, jnp.int32),
            pltpu.SMEM(clen.shape, jnp.int32),
            pltpu.VMEM(qg.shape, F32),
            pltpu.VMEM(kg.shape, F32),
            pltpu.VMEM(table.shape, F32),
            pltpu.VMEM(freq.shape, F32),
            pltpu.SemaphoreType.DMA((chunks,)),
            pltpu.SemaphoreType.DMA((chunks,)),
            pltpu.SemaphoreType.DMA((2, chunks)),
            pltpu.SemaphoreType.DMA((chunks,)),
            pltpu.SemaphoreType.DMA((3,)),
            pltpu.SemaphoreType.DMA((7,)),
        ],
        compiler_params=pltpu.CompilerParams(vmem_limit_bytes=60 * MIB),
        cost_estimate=BRIEF,
        name="prefill_%d" % which,
    )(*args)


def own_kernel(n_head, attn0, attn1, wo_hbm, own0, own1, wo_v, sems):
    width = wo_hbm.shape[1]
    nb = width // n_head
    hb = nb // 2
    head = lax.axis_index("head")
    flip_x = head + 1 - 2 * lax.rem(head, 2)
    flip_y = lax.rem(head + 2, 4)
    places = [(head * nb, 0, nb), (flip_y * nb, nb, hb), (flip_x * nb + hb, nb + hb, hb)]
    copies = [
        pltpu.make_async_copy(
            wo_hbm.at[:, pl.ds(pl.multiple_of(src, hb), size)],
            wo_v.at[:, pl.ds(dst, size)],
            sems.at[j],
        )
        for j, (src, dst, size) in enumerate(places)
    ]
    for copy in copies:
        copy.start()
    copies[0].wait()
    for attn, own in ((attn0, own0), (attn1, own1)):
        own[:, :nb] = dot(attn[...], wo_v[:, :nb]).astype(BF)
    copies[1].wait()
    copies[2].wait()
    for attn, own in ((attn0, own0), (attn1, own1)):
        own[:, nb:] = dot(attn[...], wo_v[:, nb:]).astype(BF)


def own_parts(n_head, attn0, attn1, wo):
    rows, local = attn0.shape
    nb = wo.shape[1] // n_head
    return pl.pallas_call(
        functools.partial(own_kernel, n_head),
        out_shape=[jax.ShapeDtypeStruct((rows, 2 * nb), BF)] * 2,
        in_specs=[VM, VM, HB],
        out_specs=[VM, VM],
        scratch_shapes=[pltpu.VMEM((local, 2 * nb), BF), pltpu.SemaphoreType.DMA((3,))],
        compiler_params=pltpu.CompilerParams(vmem_limit_bytes=50 * MIB),
        cost_estimate=BRIEF,
        name="own_parts",
    )(attn0, attn1, wo)


def pass_on_kernel(own, got_a, got_b, on_a, on_b):
    nb = got_a.shape[1]
    hb = nb // 2
    on_a[...] = (own[:, nb : nb + hb].astype(F32) + got_a[:, :hb].astype(F32)).astype(BF)
    on_b[...] = (own[:, nb + hb :].astype(F32) + got_b[:, :hb].astype(F32)).astype(BF)


def pass_on(p, own, got_a, got_b):
    rows, nb = got_a.shape
    return pl.pallas_call(
        pass_on_kernel,
        out_shape=[jax.ShapeDtypeStruct((rows, nb // 2), BF)] * 2,
        in_specs=[VM] * 3,
        out_specs=[VM] * 2,
        compiler_params=pltpu.CompilerParams(vmem_limit_bytes=32 * MIB),
        cost_estimate=BRIEF,
        name="pass_on_%d" % p,
    )(own, got_a, got_b)


def sum_parts(stage, own, got_a, got_b, in_a, in_b):
    hb = in_a.shape[1]
    stage[:, :hb] = (
        own[:, :hb].astype(F32) + got_a[:, hb:].astype(F32) + in_a[...].astype(F32)
    ).astype(BF)
    stage[:, hb:] = (
        own[:, hb : 2 * hb].astype(F32) + got_b[:, hb:].astype(F32) + in_b[...].astype(F32)
    ).astype(BF)


def finish_first_kernel(p, own, got_a, got_b, in_a, in_b, moved, out, handed, stage, sems):
    keep = pltpu.make_async_copy(moved, handed, sems.at[1])
    keep.start()
    sum_parts(stage, own, got_a, got_b, in_a, in_b)
    copy = pltpu.make_async_copy(stage, out.at[p], sems.at[0])
    copy.start()
    copy.wait()
    keep.wait()


def finish_first(p, prompts, own, got_a, got_b, in_a, in_b, moved):
    rows, nb = got_a.shape
    return pl.pallas_call(
        functools.partial(finish_first_kernel, p),
        out_shape=[
            jax.ShapeDtypeStruct((prompts, rows, nb), BF),
            jax.ShapeDtypeStruct(moved.shape, BF),
        ],
        in_specs=[VM] * 6,
        out_specs=[HB] * 2,
        scratch_shapes=[pltpu.VMEM((rows, nb), BF), pltpu.SemaphoreType.DMA((2,))],
        compiler_params=pltpu.CompilerParams(vmem_limit_bytes=32 * MIB),
        cost_estimate=BRIEF,
        name="finish_%d" % p,
    )(own, got_a, got_b, in_a, in_b, moved)


def finish_last_kernel(p, slots, own, got_a, got_b, in_a, in_b, mine, *refs):
    others, (_, out, dec_out, stage, sem) = refs[:-5], refs[-5:]
    sum_parts(stage, own, got_a, got_b, in_a, in_b)
    copy = pltpu.make_async_copy(stage, out.at[p], sem)
    copy.start()
    total = mine[...].astype(F32)
    for other in others:
        total = total + other[...].astype(F32)
    for t in range(dec_out.shape[0]):
        dec_out[t] = total[t * slots : (t + 1) * slots].astype(BF)
    copy.wait()


def finish_last(p, steps, slots, own, got_a, got_b, in_a, in_b, pieces, partial):
    rows, nb = got_a.shape
    return pl.pallas_call(
        functools.partial(finish_last_kernel, p, slots),
        out_shape=[
            jax.ShapeDtypeStruct(partial.shape, BF),
            jax.ShapeDtypeStruct((steps, slots, nb), BF),
        ],
        in_specs=[VM] * (5 + len(pieces)) + [HB],
        out_specs=[HB, VM],
        scratch_shapes=[pltpu.VMEM((rows, nb), BF), pltpu.SemaphoreType.DMA],
        input_output_aliases={5 + len(pieces): 0},
        compiler_params=pltpu.CompilerParams(vmem_limit_bytes=32 * MIB),
        cost_estimate=BRIEF,
        name="finish_%d" % p,
    )(own, got_a, got_b, in_a, in_b, *pieces, partial)


def decode_kernel(n_seq, plen, adm, clen, dq, dkv, cache, *refs):
    kvs, (part, handed) = refs[:-2], refs[-2:]
    seq = lax.axis_index("seq")
    slots, width = cache.shape[0], cache.shape[1]
    queries = dq[...]
    count = queries.shape[0]
    dec_rows = dkv.shape[0]
    rows = kvs[0].shape[0]
    each = rows // n_seq

    row = lax.rem(lax.broadcasted_iota(jnp.int32, (count, 1), 0), dec_rows)
    slot, step = lax.rem(row, slots), row // slots
    taken = by_slot(slot, [adm[r] for r in range(slots)])
    scores, masks, values = [], [], []
    at = lax.broadcasted_iota(jnp.int32, (1, width), 1) * n_seq + seq
    for r in range(slots):
        limit = jnp.where(adm[r] >= 0, 0, clen[r])
        masks.append((slot == r) & (at < limit))
        scores.append(dot_nt(queries, cache[r, :, :HD]))
        values.append(cache[r, :, HD:])
    spot = lax.broadcasted_iota(jnp.int32, (1, rows), 1)
    for p, kv in enumerate(kvs):
        prompt = seq * len(kvs) + p
        masks.append((taken == prompt) & (spot < plen[prompt]))
        scores.append(dot_nt(queries, kv[:, :HD]))
        values.append(kv[:, HD:])
    other = lax.broadcasted_iota(jnp.int32, (1, dec_rows), 1)
    first = jnp.where(seq == 0, 1, 0)
    masks.append(
        (lax.rem(other, slots) == slot) & (other // slots <= step) & (first + 0 * other > 0)
    )
    scores.append(dot_nt(queries, dkv[:, :HD]))
    values.append(dkv[:, HD:])

    top = jnp.full((count, 1), NEG, F32)
    scores = [jnp.where(mask, score, NEG) for mask, score in zip(masks, scores)]
    for score in scores:
        top = jnp.maximum(top, jnp.max(score, axis=-1, keepdims=True))
    total = jnp.zeros((count, 1), F32)
    acc = jnp.zeros((count, HD), F32)
    for mask, score, value in zip(masks, scores, values):
        expo = jnp.where(mask, jnp.exp2((score - top) * C2), 0.0)
        total = total + jnp.sum(expo, axis=-1, keepdims=True)
        acc = acc + dot(expo.astype(BF), value)
    some = total > 0.0
    safe = jnp.where(some, total, 1.0)
    part[:count, :] = acc * (1.0 / safe)
    level = jnp.where(some, top * C2 + jnp.log2(safe), NEG)
    eye = lax.broadcasted_iota(jnp.int32, (count, count), 0) == lax.broadcasted_iota(
        jnp.int32, (count, count), 1
    )
    part[count : count + 1, :] = jnp.sum(jnp.where(eye, level, 0.0), axis=0, keepdims=True)

    new = lax.broadcasted_iota(jnp.int32, (rows, rows), 0)
    old = lax.broadcasted_iota(jnp.int32, (rows, rows), 1)
    move = jnp.where(old == lax.rem(new, each) * n_seq + new // each, 1.0, 0.0).astype(BF)
    for p, kv in enumerate(kvs):
        handed[p] = dot(move, kv[...]).astype(BF)


def decode_attention(n_seq, plen, adm, clen, dq, dkv, cache, kvs):
    count = dq.shape[0]
    rows = kvs[0].shape[0]
    return pl.pallas_call(
        functools.partial(decode_kernel, n_seq),
        out_shape=[
            jax.ShapeDtypeStruct((count + 8, HD), F32),
            jax.ShapeDtypeStruct((len(kvs), rows, 2 * HD), BF),
        ],
        in_specs=[SM] * 3 + [VM] * (3 + len(kvs)),
        out_specs=[VM] * 2,
        compiler_params=pltpu.CompilerParams(vmem_limit_bytes=60 * MIB),
        cost_estimate=BRIEF,
        name="decode_attention",
    )(plen, adm, clen, dq, dkv, cache, *kvs)


def joined(bit, mine, other):
    count = mine.shape[0] - 8
    swap = lax.rem(lax.axis_index("seq") // bit, 2) == 1
    one, two = mine[...], other[...]
    low = jnp.where(swap, two, one)
    high = jnp.where(swap, one, two)
    eye = lax.broadcasted_iota(jnp.int32, (count, count), 0) == lax.broadcasted_iota(
        jnp.int32, (count, count), 1
    )

    def column(row):
        return jnp.sum(jnp.where(eye, row, 0.0), axis=1, keepdims=True)

    row_a, row_b = low[count : count + 1, :], high[count : count + 1, :]
    best = jnp.maximum(row_a, row_b)
    scale_a, scale_b = jnp.exp2(row_a - best), jnp.exp2(row_b - best)
    total = scale_a + scale_b
    inverse = 1.0 / total
    mixed = low[:count] * column(scale_a * inverse) + high[:count] * column(scale_b * inverse)
    return mixed, best + jnp.log2(total)


def join_kernel(bit, mine, other, out):
    count = mine.shape[0] - 8
    mixed, level = joined(bit, mine, other)
    out[:count, :] = mixed
    out[count : count + 1, :] = level


def join(bit, mine, other):
    return pl.pallas_call(
        functools.partial(join_kernel, bit),
        out_shape=jax.ShapeDtypeStruct(mine.shape, F32),
        in_specs=[VM, VM],
        out_specs=VM,
        cost_estimate=BRIEF,
        name="join_%d" % bit,
    )(mine, other)


def decode_out_kernel(bit, n_head, mine, other, wo_hbm, *refs):
    outs, (wo_v, sems) = refs[:n_head], refs[n_head:]
    count = mine.shape[0] - 8
    rows = outs[0].shape[0]
    nb = outs[0].shape[1]
    head = lax.axis_index("head")
    flip_x = head + 1 - 2 * lax.rem(head, 2)
    flip_y = lax.rem(head + 2, 4)
    copies = [
        pltpu.make_async_copy(
            wo_hbm.at[:, pl.ds(pl.multiple_of(dest * nb, nb), nb)], wo_v.at[d], sems.at[d]
        )
        for d, dest in enumerate((head, flip_x, flip_y, 3 - head))
    ]
    for copy in reversed(copies):
        copy.start()
    mixed, _ = joined(bit, mine, other)
    mixed = mixed.astype(BF)
    flat = jnp.concatenate([mixed[i * rows : (i + 1) * rows] for i in range(count // rows)], axis=1)
    for d in reversed(range(n_head)):
        copies[d].wait()
        outs[d][...] = dot(flat, wo_v[d]).astype(BF)


def decode_project(bit, n_head, dec_rows, mine, other, wo):
    local, width = wo.shape
    nb = width // n_head
    return pl.pallas_call(
        functools.partial(decode_out_kernel, bit, n_head),
        out_shape=[jax.ShapeDtypeStruct((dec_rows, nb), BF)] * n_head,
        in_specs=[VM, VM, HB],
        out_specs=[VM] * n_head,
        scratch_shapes=[pltpu.VMEM((n_head, local, nb), BF), pltpu.SemaphoreType.DMA((n_head,))],
        compiler_params=pltpu.CompilerParams(vmem_limit_bytes=50 * MIB),
        cost_estimate=BRIEF,
        name="decode_project",
    )(mine, other, wo)


def local(
    prompts, prompt_len, admitted, cache_len, cache_kv, dec_tokens, w_query, w_key, w_value, w_out, q_gain, k_gain
):
    n_seq = lax.axis_size("seq")
    n_head = lax.axis_size("head")
    pr_dev, rows, width = prompts.shape
    steps, slots, _ = dec_tokens.shape
    nb = width // n_head
    qg, kg = q_gain.reshape(1, HD), k_gain.reshape(1, HD)
    table = jnp.asarray(prompt_table(rows))
    freq = jnp.asarray(np.tile(frequencies(), 2)[None, :])
    scalars = (prompt_len, admitted, cache_len)
    weights = (w_query, w_key, w_value, w_out, qg, kg, table, freq)

    across_x = [(i, i ^ 1) for i in range(n_head)]
    across_y = [(i, i ^ 2) for i in range(n_head)]
    across_xy = [(i, i ^ 3) for i in range(n_head)]

    def head_move(value, pairs):
        return lax.ppermute(value, "head", pairs)

    got, attns, kvs = [None] * pr_dev, [None] * pr_dev, [None] * pr_dev
    for p in reversed(range(pr_dev)):
        dec = dec_tokens
        if p < pr_dev - 1:
            dec = lax.optimization_barrier((dec_tokens, kvs[p + 1]))[0]
        dec = dec.reshape(steps * slots, width)
        out = prefill(p, p == 0, n_head, *scalars, prompts, dec, *weights)
        got[p] = (head_move(out[0], across_x), head_move(out[1], across_y))
        attns[p], kvs[p] = out[2], out[3]
    dq, dkv = out[4], out[5]
    part, handed = decode_attention(n_seq, *scalars, dq, dkv, cache_kv[0], kvs)
    own = own_parts(n_head, *attns, w_out)

    sums = [None] * pr_dev

    def after(value, other):
        return lax.optimization_barrier((value, other))[0]

    def send_on(p, before=None):
        if before is not None:
            got[p] = (after(got[p][0], before), got[p][1])
        on_a, on_b = pass_on(p, own[p], *got[p])
        sums[p] = (own[p], *got[p], head_move(on_a, across_y), head_move(on_b, across_x))
        return on_a

    def hand_over():
        each = rows // n_seq
        sending = handed.reshape(pr_dev, n_seq, each, 2 * HD)
        moved = lax.all_to_all(sending, "seq", split_axis=1, concat_axis=0, tiled=True)
        return moved.reshape(1, pr_dev * n_seq, each, 2 * HD)

    bit = 1
    while bit < n_seq:
        other = lax.ppermute(part, "seq", [(i, i ^ bit) for i in range(n_seq)])
        if bit == 1:
            other = after(other, send_on(1))
        if bit == 2:
            moved = hand_over()
            other = after(other, moved)
        if 2 * bit < n_seq:
            part = join(bit, part, other)
        else:
            other = after(other, send_on(0, part))
            partial, handed_out = finish_first(1, pr_dev, *sums[1], moved)
            other = after(other, partial)
            pieces = decode_project(bit, n_head, steps * slots, part, other, w_out)
        bit *= 2
    pieces = [pieces[0]] + [
        head_move(piece, pairs)
        for piece, pairs in zip(pieces[1:], (across_x, across_y, across_xy))
    ]
    prefill_out, decode_out = finish_last(0, steps, slots, *sums[0], pieces, partial)
    return (prefill_out, handed_out, decode_out)


def solution(mesh):
    placed = (
        P("seq", None, None),
        P(),
        P(),
        P(),
        P("head", None, "seq", None),
        P(),
        P(None, "head"),
        P(None, "head"),
        P(None, "head"),
        P("head", None),
        P(),
        P(),
    )
    return jax.shard_map(
        local,
        mesh=mesh,
        in_specs=placed,
        out_specs=(P("seq", None, "head"), P("head", None, "seq", None), P(None, None, "head")),
        check_vma=False,
    )
```

time: 103 us -> 85.5 us (0.83)
  other arithmetic: 10.6 us -> 0 us
  local copies, waits for them, and re-layouts: 18 us -> 7.98 us
  waiting for transfers between devices: 10.9 us -> 5.29 us
  Pallas kernels: 40.4 us -> 45.9 us
  starting transfers between devices: 21.5 us -> 24.9 us
    unnamed x55 -> x16, local copies, waits for them, and re-layouts: 15.7 us -> 5.64 us
    ppermute x11, waiting for transfers between devices: 10.2 us -> 2.51 us  [head_move(): return lax.ppermute(value, 'head', pairs)]
    convert_element_type x7 -> x0, other arithmetic: 7.21 us -> none  [the longest x4 4.97 us: local(): a, b = (a.astype(F32), b.astype(F32))]
    pallas_call x0 -> x4, Pallas kernels: none -> 6.28 us  [the longest x1 2.8 us: finish_last(): pl.pallas_call(functools.partial(finish_last_kernel, p, slots), out_shape...]
    pallas_call x2, Pallas kernels: 30.6 us -> 25 us  [prefill(): pl.pallas_call(functools.partial(prefill_kernel, which, dec_rows, slots,...]
    pallas_call x1, Pallas kernels: 1.27 us -> 3.92 us  [decode_project(): pl.pallas_call(functools.partial(decode_out_kernel, bit, n_head), out_sha...]
    ppermute x11, starting transfers between devices: 12.3 us -> 14.7 us  [head_move(): return lax.ppermute(value, 'head', pairs)]
    concatenate x1 -> x0, other arithmetic: 2.28 us -> none  [local(): jnp.concatenate([own_keep[p, :, :hb] + a[:, hb:] + on_a.astype(F32), own_...]
  transfers between devices with their start and end apart: 15 -> 15, of which waited for: 4 -> 4; matrix products, arithmetic and copies ran while one was open for 8% -> 3% of each run, Pallas kernels for 8% -> 36%
where the time goes in v2:
time: 85.5 us; the launch traced here: 84.9 us
  Pallas kernels  45.9 us (54%)
  starting transfers between devices  24.9 us (29%)
  local copies, waits for them, and re-layouts  7.98 us (9%)
  waiting for transfers between devices  5.29 us (6%)
  between operations  0.91 us (1%)
    pallas_call x2, Pallas kernels, prefill(): pl.pallas_call(functools.partial(prefill_kernel, which, dec_rows, slots,...  25 us
    ppermute x11, starting transfers between devices, head_move(): return lax.ppermute(value, 'head', pairs)  14.7 us
    unnamed x16, local copies, waits for them, and re-layouts  5.64 us
    all_to_all x1, starting transfers between devices, hand_over(): lax.all_to_all(sending, 'seq', split_axis=1, concat_axis=0, tiled=True)  5.33 us
    ppermute x3, starting transfers between devices, local(): other = lax.ppermute(part, 'seq', [(i, i ^ bit) for i in range(n_seq)])  4.83 us
    pallas_call x1, Pallas kernels, own_parts(): pl.pallas_call(functools.partial(own_kernel, n_head), out_shape=[jax.Shap...  4.12 us
    pallas_call x1, Pallas kernels, decode_project(): pl.pallas_call(functools.partial(decode_out_kernel, bit, n_head), out_sha...  3.92 us
    pallas_call x2, Pallas kernels, join(): pl.pallas_call(functools.partial(join_kernel, bit), out_shape=jax.ShapeDt...  3.34 us
  transfers between devices with their start and end apart: 15, of which 4 were waited for; matrix products, arithmetic and copies ran while one was open for 3% of the time, Pallas kernels for 36%

profile of v2, /device:TPU:0, one launch (start us, length us, event | category | flops | bytes accessed | tf_op | source)
XLA Modules:
  0.0 84.9 jit_solution(6129106087473908155)
XLA Ops:
  0.6 0.0 copy-start.5
  0.6 12.4 %prefill_1.1 = (bf16[256,1024]{1,0:T(8,128)(2,1)}, bf16[256,1024]{1,0:T(8,128)(2,1)}, bf16[256,1024]{1,0:T(8,128)(2,1)}, bf16[256,256]{1,0:T(8,128)(2,1)}) custom-call(s32[16]{0:T(128)} %plen.1, s32[4]{0:T(128)} %adm.1, s32[4]{0:T(128)} %clen.1, bf16[2,256,4096]{2,1,0:T(8,128)(2,1)} %refs_3_.3, bf16[4096,1024]{1,0:T(8,128)(2,1)} %refs_5_.3, ...), custom_call_target="tpu_custom_call" | custom-call | flops 1 | bytes 1 | tf_op jit(solution)/shard_map/prefill_1/pallas_call | solution.py:224
  13.0 3.0 %collective-permute-start.2 = (bf16[256,1024]{1,0:T(8,128)(2,1)}, bf16[256,1024]{1,0:T(8,128)(2,1)S(1)}, u32[]{:S(2)}, u32[]{:S(2)}) collective-permute-start(bf16[256,1024]{1,0:T(8,128)(2,1)} %get-tuple-element.46), channel_id=1, source_target_pairs={{0,8},{8,0},{16,24},{24,16},{1,9},{9,1},{17,25},{25,17},{2,10},{10... | collective-permute-start | bytes 1572872 | tf_op jit(solution)/shard_map/ppermute | solution.py:560
  16.0 1.5 %collective-permute-start.3 = (bf16[256,1024]{1,0:T(8,128)(2,1)}, bf16[256,1024]{1,0:T(8,128)(2,1)S(1)}, u32[]{:S(2)}, u32[]{:S(2)}) collective-permute-start(bf16[256,1024]{1,0:T(8,128)(2,1)} %get-tuple-element.47), channel_id=1, source_target_pairs={{0,16},{8,24},{16,0},{24,8},{1,17},{9,25},{17,1},{25,9},{2,18},{10... | collective-permute-start | bytes 1572872 | tf_op jit(solution)/shard_map/ppermute | solution.py:560
  17.6 0.0 copy-done.5
  17.6 0.7 reshape.24.refs_4_
  18.3 12.6 %prefill_0.1 = (bf16[256,1024]{1,0:T(8,128)(2,1)}, bf16[256,1024]{1,0:T(8,128)(2,1)}, bf16[256,1024]{1,0:T(8,128)(2,1)}, bf16[256,256]{1,0:T(8,128)(2,1)}, bf16[...) custom-call(s32[16]{0:T(128)} %plen.1, s32[4]{0:T(128)} %adm.1, s32[4]{0:T(128)} %clen.1, bf16[2,256,4096]{2,1,0:T(8,128)(2,1)} %refs_3_.3, ...), custom_call_target="tpu_custom_call" | custom-call | flops 1 | bytes 1 | tf_op jit(solution)/shard_map/prefill_0/pallas_call | solution.py:224
  30.9 0.6 collective-permute-start
  31.5 0.1 collective-permute-start.5
  31.5 3.2 %decode_attention.1 = (f32[136,128]{1,0:T(8,128)}, bf16[2,256,256]{2,1,0:T(8,128)(2,1)}) custom-call(s32[16]{0:T(128)} %plen.1, s32[4]{0:T(128)} %adm.1, s32[4]{0:T(128)} %clen.1, bf16[128,128]{1,0:T(8,128)(2,1)} %get-tuple-element.41.dq, bf16[16,256]{1,0:T(8,128)(2,1)} %get-tuple-element.42.dkv, bf16[4,512,256]{2,1,0:T(8,128)(2,1)} %bitcast.10, ...), custom_call_target="tpu_custom_call" | custom-call | flops 1 | bytes 1 | tf_op jit(solution)/shard_map/decode_attention/pallas_call | solution.py:448
  34.7 1.7 %copy.18 = bf16[2,8,32,256]{3,2,0,1:T(8,128)(2,1)} copy(bf16[2,8,32,256]{3,2,1,0:T(8,128)(2,1)} %bitcast.11) | data formatting | bytes 524288 | tf_op jit(solution)/shard_map/reshape | solution.py:589
  36.4 5.3 %all-to-all-start = ((bf16[2,8,32,256]{3,2,0,1:T(8,128)(2,1)}), bf16[2,8,32,256]{3,2,0,1:T(8,128)(2,1)S(1)}, u32[]{:S(2)}, u32[]{:S(2)}) async-start(bf16[2,8,32,256]{3,2,0,1:T(8,128)(2,1)} %copy.18), calls=%async_computation | async-start | bytes 524288 | tf_op jit(solution)/shard_map/all_to_all | solution.py:590
  41.7 0.5 collective-permute-start.1
  42.2 0.0 copy-start
  42.2 1.0 %copy-done = bf16[256,1024]{1,0:T(8,128)(2,1)S(1)} copy-done((bf16[256,1024]{1,0:T(8,128)(2,1)S(1)}, bf16[256,1024]{1,0:T(8,128)(2,1)}, u32[]{:S(2)}) %copy-start) | copy-done | bytes 524312
  43.3 0.0 copy-start.1
  43.3 1.0 %copy-done.1 = bf16[256,1024]{1,0:T(8,128)(2,1)S(1)} copy-done((bf16[256,1024]{1,0:T(8,128)(2,1)S(1)}, bf16[256,1024]{1,0:T(8,128)(2,1)}, u32[]{:S(2)}) %copy-start.1) | copy-done | bytes 524312
  44.3 4.1 %own_parts.1 = (bf16[256,2048]{1,0:T(8,128)(2,1)S(1)}, bf16[256,2048]{1,0:T(8,128)(2,1)S(1)}) custom-call(bf16[256,1024]{1,0:T(8,128)(2,1)S(1)} %copy-done.1, bf16[256,1024]{1,0:T(8,128)(2,1)S(1)} %copy-done, bf16[1024,4096]{1,0:T(8,128)(2,1)} %wo_hbm.3), custom_call_target="tpu_custom_call" | custom-call | flops 1 | bytes 1 | tf_op jit(solution)/shard_map/own_parts/pallas_call | solution.py:285
  48.4 0.0 collective-permute-done.2.got_a
  48.5 0.0 collective-permute-done.3.got_b
  48.5 0.1 pass_on_1.1
  48.6 0.0 copy-start.3
  48.6 0.7 copy-done.3
  49.3 0.0 copy-start.4
  49.3 0.7 copy-done.4
  50.0 0.0 collective-permute-done.1.other
  50.0 0.0 copy-start.6
  50.0 0.6 copy-done.6
  50.7 1.7 %join_1.1.mine = f32[136,128]{1,0:T(8,128)} custom-call(f32[136,128]{1,0:T(8,128)} %get-tuple-element.44.mine, f32[136,128]{1,0:T(8,128)} %copy-done.6), custom_call_target="tpu_custom_call" | custom-call | flops 1 | bytes 1 | tf_op jit(solution)/shard_map/join_1/pallas_call | solution.py:492
  52.3 1.7 %collective-permute-start.4 = (f32[136,128]{1,0:T(8,128)}, f32[136,128]{1,0:T(8,128)S(1)}, u32[]{:S(2)}, u32[]{:S(2)}) collective-permute-start(f32[136,128]{1,0:T(8,128)} %join_1.1.mine), channel_id=1, source_target_pairs={{0,2},{1,3},{2,0},{3,1},{4,6},{5,7},{6,4},{7,5},{8,10},{9,11},{10,... | collective-permute-start | bytes 208904 | tf_op jit(solution)/shard_map/ppermute | solution.py:595
  54.0 1.5 %collective-permute-start.10 = (bf16[256,512]{1,0:T(8,128)(2,1)}, bf16[256,512]{1,0:T(8,128)(2,1)}, u32[]{:S(2)}, u32[]{:S(2)}) collective-permute-start(bf16[256,512]{1,0:T(8,128)(2,1)} %copy-done.4), channel_id=1, source_target_pairs={{0,8},{8,0},{16,24},{24,16},{1,9},{9,1},{17,25},{25,17},{2,10},{10... | collective-permute-start | bytes 786440 | tf_op jit(solution)/shard_map/ppermute | solution.py:560
  55.5 1.5 %collective-permute-start.9 = (bf16[256,512]{1,0:T(8,128)(2,1)}, bf16[256,512]{1,0:T(8,128)(2,1)}, u32[]{:S(2)}, u32[]{:S(2)}) collective-permute-start(bf16[256,512]{1,0:T(8,128)(2,1)} %copy-done.3), channel_id=1, source_target_pairs={{0,16},{8,24},{16,0},{24,8},{1,17},{9,25},{17,1},{25,9},{2,18},{10... | collective-permute-start | bytes 786440 | tf_op jit(solution)/shard_map/ppermute | solution.py:560
  57.0 0.0 all-to-all-done
  57.0 0.0 collective-permute-done.4.other
  57.0 0.0 copy-start.7
  57.0 0.6 copy-done.7
  57.6 1.7 %join_2.1.mine = f32[136,128]{1,0:T(8,128)} custom-call(f32[136,128]{1,0:T(8,128)} %join_1.1.mine, f32[136,128]{1,0:T(8,128)} %copy-done.7), custom_call_target="tpu_custom_call" | custom-call | flops 1 | bytes 1 | tf_op jit(solution)/shard_map/join_2/pallas_call | solution.py:492
  59.3 0.0 collective-permute-done.got_a
  59.3 0.0 collective-permute-done.5.got_b
  59.3 1.3 %pass_on_0.1 = (bf16[256,512]{1,0:T(8,128)(2,1)S(1)}, bf16[256,512]{1,0:T(8,128)(2,1)S(1)}) custom-call(bf16[256,2048]{1,0:T(8,128)(2,1)S(1)} %get-tuple-element.39.own, bf16[256,1024]{1,0:T(8,128)(2,1)} %collective-permute-done.got_a, bf16[256,1024]{1,0:T(8,128)(2,1)} %collective-permute-done.5.got_b), custom_call_target="tpu_custom_call" | custom-call | flops 1 | bytes 1 | tf_op jit(solution)/shard_map/pass_on_0/pallas_call | solution.py:306
  60.6 1.4 %collective-permute-start.7 = (bf16[256,512]{1,0:T(8,128)(2,1)S(1)}, bf16[256,512]{1,0:T(8,128)(2,1)S(1)}, u32[]{:S(2)}, u32[]{:S(2)}) collective-permute-start(bf16[256,512]{1,0:T(8,128)(2,1)S(1)} %get-tuple-element.55), channel_id=1, source_target_pairs={{0,8},{8,0},{16,24},{24,16},{1,9},{9,1},{17,25},{25,17},{2,10},{10... | collective-permute-start | bytes 786440 | tf_op jit(solution)/shard_map/ppermute | solution.py:560
  62.1 1.5 %collective-permute-start.6 = (bf16[256,512]{1,0:T(8,128)(2,1)S(1)}, bf16[256,512]{1,0:T(8,128)(2,1)S(1)}, u32[]{:S(2)}, u32[]{:S(2)}) collective-permute-start(bf16[256,512]{1,0:T(8,128)(2,1)S(1)} %get-tuple-element.54), channel_id=1, source_target_pairs={{0,16},{8,24},{16,0},{24,8},{1,17},{9,25},{17,1},{25,9},{2,18},{10... | collective-permute-start | bytes 786440 | tf_op jit(solution)/shard_map/ppermute | solution.py:560
  63.6 2.6 %collective-permute-start.8 = (f32[136,128]{1,0:T(8,128)}, f32[136,128]{1,0:T(8,128)S(1)}, u32[]{:S(2)}, u32[]{:S(2)}) collective-permute-start(f32[136,128]{1,0:T(8,128)} %join_2.1.mine), channel_id=1, source_target_pairs={{0,4},{1,5},{2,6},{3,7},{4,0},{5,1},{6,2},{7,3},{8,12},{9,13},{10,... | collective-permute-start | bytes 208904 | tf_op jit(solution)/shard_map/ppermute | solution.py:595
  66.2 2.8 %collective-permute-done.8.other = f32[136,128]{1,0:T(8,128)S(1)} collective-permute-done((f32[136,128]{1,0:T(8,128)}, f32[136,128]{1,0:T(8,128)S(1)}, u32[]{:S(2)}, u32[]{:S(2)}) %collective-permute-start.8) | collective-permute-done | bytes 69664 | tf_op jit(solution)/shard_map/ppermute | solution.py:595
  69.0 0.0 collective-permute-done.10.in_b
  69.0 0.0 collective-permute-done.9.in_a
  69.0 2.0 %finish_1.1 = (bf16[2,256,1024]{2,1,0:T(8,128)(2,1)}, bf16[1,16,32,256]{3,2,1,0:T(8,128)(2,1)}) custom-call(bf16[256,2048]{1,0:T(8,128)(2,1)S(1)} %get-tuple-element.45.own, bf16[256,1024]{1,0:T(8,128)(2,1)S(1)} %collective-permute-done.2.got_a, bf16[256,1024]{1,0:T(8,128)(2,1)S(1)} %collective-permute-done.3.got_b, ...), custom_call_target="tpu_custom_call" | custom-call | flops 1 | bytes 1 | tf_op jit(solution)/shard_map/finish_1/pallas_call | solution.py:339
  71.1 0.0 copy-start.2
  71.1 0.9 %copy-done.2 = f32[136,128]{1,0:T(8,128)S(1)} copy-done((f32[136,128]{1,0:T(8,128)S(1)}, f32[136,128]{1,0:T(8,128)}, u32[]{:S(2)}) %copy-start.2) | copy-done | bytes 69656
  72.0 3.9 %decode_project.1 = (bf16[16,1024]{1,0:T(8,128)(2,1)S(1)}, bf16[16,1024]{1,0:T(8,128)(2,1)S(1)}, bf16[16,1024]{1,0:T(8,128)(2,1)S(1)}, bf16[16,1024]{1,0:T(8,128)(2,1)S(1)}) custom-call(f32[136,128]{1,0:T(8,128)S(1)} %copy-done.2, f32[136,128]{1,0:T(8,128)S(1)} %collective-permute-done.8.other, bf16[1024,4096]{1,0:T(8,128)(2,1)} %wo_hbm.3), custom_call_target="tpu_custom_call" | custom-call | flops 1 | bytes 1 | tf_op jit(solution)/shard_map/decode_project/pallas_call | solution.py:529
  75.9 0.6 collective-permute-start.11
  76.5 0.6 collective-permute-start.12
  77.1 2.3 %collective-permute-start.13 = (bf16[16,1024]{1,0:T(8,128)(2,1)S(1)}, bf16[16,1024]{1,0:T(8,128)(2,1)S(1)}, u32[]{:S(2)}, u32[]{:S(2)}) collective-permute-start(bf16[16,1024]{1,0:T(8,128)(2,1)S(1)} %get-tuple-element.63), channel_id=1, source_target_pairs={{0,24},{8,16},{16,8},{24,0},{1,25},{9,17},{17,9},{25,1},{2,26},{10... | collective-permute-start | bytes 98312 | tf_op jit(solution)/shard_map/ppermute | solution.py:560
  79.4 0.4 collective-permute-done.11.refs_0_
  79.9 0.5 collective-permute-done.12.refs_1_
  80.4 1.5 %collective-permute-done.13.refs_2_ = bf16[16,1024]{1,0:T(8,128)(2,1)S(1)} collective-permute-done((bf16[16,1024]{1,0:T(8,128)(2,1)S(1)}, bf16[16,1024]{1,0:T(8,128)(2,1)S(1)}, u32[]{:S(2)}, u32[]{:S(2)}) %collective-permute-start.13) | collective-permute-done | bytes 32800 | tf_op jit(solution)/shard_map/ppermute | solution.py:560
  81.9 0.0 collective-permute-done.7.in_b
  81.9 0.0 collective-permute-done.6.in_a
  81.9 2.8 %finish_0.1 = (bf16[2,256,1024]{2,1,0:T(8,128)(2,1)}, bf16[4,4,1024]{2,1,0:T(4,128)(2,1)}) custom-call(bf16[256,2048]{1,0:T(8,128)(2,1)S(1)} %get-tuple-element.39.own, bf16[256,1024]{1,0:T(8,128)(2,1)} %collective-permute-done.got_a, bf16[256,1024]{1,0:T(8,128)(2,1)} %collective-permute-done.5.got_b, ...), custom_call_target="tpu_custom_call", output_to_operand_aliasing={{0}: (9, {})} | custom-call | flops 1 | bytes 1 | tf_op jit(solution)/shard_map/finish_0/pallas_call | solution.py:369
Async XLA Ops:
  0.6 16.9 %copy-start.5 = (bf16[4,4,4096]{2,1,0:T(4,128)(2,1)S(1)}, bf16[4,4,4096]{2,1,0:T(4,128)(2,1)}, u32[]{:S(2)}) copy-start(bf16[4,4,4096]{2,1,0:T(4,128)(2,1)} %param.19) | copy-start | bytes 393220
  13.0 35.4 %collective-permute-start.2 = (bf16[256,1024]{1,0:T(8,128)(2,1)}, bf16[256,1024]{1,0:T(8,128)(2,1)S(1)}, u32[]{:S(2)}, u32[]{:S(2)}) collective-permute-start(bf16[256,1024]{1,0:T(8,128)(2,1)} %get-tuple-element.46), channel_id=1, source_target_pairs={{0,8},{8,0},{16,24},{24,16},{1,9},{9,1},{17,25},{25,17},{2,10},{10... | collective-permute-start | bytes 1572872 | tf_op jit(solution)/shard_map/ppermute | solution.py:560
  16.0 32.4 %collective-permute-start.3 = (bf16[256,1024]{1,0:T(8,128)(2,1)}, bf16[256,1024]{1,0:T(8,128)(2,1)S(1)}, u32[]{:S(2)}, u32[]{:S(2)}) collective-permute-start(bf16[256,1024]{1,0:T(8,128)(2,1)} %get-tuple-element.47), channel_id=1, source_target_pairs={{0,16},{8,24},{16,0},{24,8},{1,17},{9,25},{17,1},{25,9},{2,18},{10... | collective-permute-start | bytes 1572872 | tf_op jit(solution)/shard_map/ppermute | solution.py:560
  30.9 28.5 %collective-permute-start = (bf16[256,1024]{1,0:T(8,128)(2,1)}, bf16[256,1024]{1,0:T(8,128)(2,1)}, u32[]{:S(2)}, u32[]{:S(2)}) collective-permute-start(bf16[256,1024]{1,0:T(8,128)(2,1)} %get-tuple-element.40), channel_id=1, source_target_pairs={{0,8},{8,0},{16,24},{24,16},{1,9},{9,1},{17,25},{25,17},{2,10},{10... | collective-permute-start | bytes 1572872 | tf_op jit(solution)/shard_map/ppermute | solution.py:560
  31.5 27.9 %collective-permute-start.5 = (bf16[256,1024]{1,0:T(8,128)(2,1)}, bf16[256,1024]{1,0:T(8,128)(2,1)}, u32[]{:S(2)}, u32[]{:S(2)}) collective-permute-start(bf16[256,1024]{1,0:T(8,128)(2,1)} %get-tuple-element.53), channel_id=1, source_target_pairs={{0,16},{8,24},{16,0},{24,8},{1,17},{9,25},{17,1},{25,9},{2,18},{10... | collective-permute-start | bytes 1572872 | tf_op jit(solution)/shard_map/ppermute | solution.py:560
  36.4 20.6 %all-to-all-start = ((bf16[2,8,32,256]{3,2,0,1:T(8,128)(2,1)}), bf16[2,8,32,256]{3,2,0,1:T(8,128)(2,1)S(1)}, u32[]{:S(2)}, u32[]{:S(2)}) async-start(bf16[2,8,32,256]{3,2,0,1:T(8,128)(2,1)} %copy.18), calls=%async_computation | async-start | bytes 524288 | tf_op jit(solution)/shard_map/all_to_all | solution.py:590
  41.7 8.3 %collective-permute-start.1 = (f32[136,128]{1,0:T(8,128)}, f32[136,128]{1,0:T(8,128)S(1)}, u32[]{:S(2)}, u32[]{:S(2)}) collective-permute-start(f32[136,128]{1,0:T(8,128)} %get-tuple-element.44.mine), channel_id=1, source_target_pairs={{0,1},{1,0},{2,3},{3,2},{4,5},{5,4},{6,7},{7,6},{8,9},{9,8},{10,11... | collective-permute-start | bytes 208904 | tf_op jit(solution)/shard_map/ppermute | solution.py:595
  42.2 1.0 %copy-start = (bf16[256,1024]{1,0:T(8,128)(2,1)S(1)}, bf16[256,1024]{1,0:T(8,128)(2,1)}, u32[]{:S(2)}) copy-start(bf16[256,1024]{1,0:T(8,128)(2,1)} %get-tuple-element.38.attn1) | copy-start | bytes 1572868
  43.3 1.0 %copy-start.1 = (bf16[256,1024]{1,0:T(8,128)(2,1)S(1)}, bf16[256,1024]{1,0:T(8,128)(2,1)}, u32[]{:S(2)}) copy-start(bf16[256,1024]{1,0:T(8,128)(2,1)} %get-tuple-element.37.attn0) | copy-start | bytes 1572868
  48.6 0.7 copy-start.3
  49.3 0.7 copy-start.4
  50.0 0.6 copy-start.6
  52.3 4.7 %collective-permute-start.4 = (f32[136,128]{1,0:T(8,128)}, f32[136,128]{1,0:T(8,128)S(1)}, u32[]{:S(2)}, u32[]{:S(2)}) collective-permute-start(f32[136,128]{1,0:T(8,128)} %join_1.1.mine), channel_id=1, source_target_pairs={{0,2},{1,3},{2,0},{3,1},{4,6},{5,7},{6,4},{7,5},{8,10},{9,11},{10,... | collective-permute-start | bytes 208904 | tf_op jit(solution)/shard_map/ppermute | solution.py:595
  54.0 15.0 %collective-permute-start.10 = (bf16[256,512]{1,0:T(8,128)(2,1)}, bf16[256,512]{1,0:T(8,128)(2,1)}, u32[]{:S(2)}, u32[]{:S(2)}) collective-permute-start(bf16[256,512]{1,0:T(8,128)(2,1)} %copy-done.4), channel_id=1, source_target_pairs={{0,8},{8,0},{16,24},{24,16},{1,9},{9,1},{17,25},{25,17},{2,10},{10... | collective-permute-start | bytes 786440 | tf_op jit(solution)/shard_map/ppermute | solution.py:560
  55.5 13.5 %collective-permute-start.9 = (bf16[256,512]{1,0:T(8,128)(2,1)}, bf16[256,512]{1,0:T(8,128)(2,1)}, u32[]{:S(2)}, u32[]{:S(2)}) collective-permute-start(bf16[256,512]{1,0:T(8,128)(2,1)} %copy-done.3), channel_id=1, source_target_pairs={{0,16},{8,24},{16,0},{24,8},{1,17},{9,25},{17,1},{25,9},{2,18},{10... | collective-permute-start | bytes 786440 | tf_op jit(solution)/shard_map/ppermute | solution.py:560
  57.0 0.6 copy-start.7
  60.6 21.3 %collective-permute-start.7 = (bf16[256,512]{1,0:T(8,128)(2,1)S(1)}, bf16[256,512]{1,0:T(8,128)(2,1)S(1)}, u32[]{:S(2)}, u32[]{:S(2)}) collective-permute-start(bf16[256,512]{1,0:T(8,128)(2,1)S(1)} %get-tuple-element.55), channel_id=1, source_target_pairs={{0,8},{8,0},{16,24},{24,16},{1,9},{9,1},{17,25},{25,17},{2,10},{10... | collective-permute-start | bytes 786440 | tf_op jit(solution)/shard_map/ppermute | solution.py:560
  62.1 19.8 %collective-permute-start.6 = (bf16[256,512]{1,0:T(8,128)(2,1)S(1)}, bf16[256,512]{1,0:T(8,128)(2,1)S(1)}, u32[]{:S(2)}, u32[]{:S(2)}) collective-permute-start(bf16[256,512]{1,0:T(8,128)(2,1)S(1)} %get-tuple-element.54), channel_id=1, source_target_pairs={{0,16},{8,24},{16,0},{24,8},{1,17},{9,25},{17,1},{25,9},{2,18},{10... | collective-permute-start | bytes 786440 | tf_op jit(solution)/shard_map/ppermute | solution.py:560
  63.6 5.4 %collective-permute-start.8 = (f32[136,128]{1,0:T(8,128)}, f32[136,128]{1,0:T(8,128)S(1)}, u32[]{:S(2)}, u32[]{:S(2)}) collective-permute-start(f32[136,128]{1,0:T(8,128)} %join_2.1.mine), channel_id=1, source_target_pairs={{0,4},{1,5},{2,6},{3,7},{4,0},{5,1},{6,2},{7,3},{8,12},{9,13},{10,... | collective-permute-start | bytes 208904 | tf_op jit(solution)/shard_map/ppermute | solution.py:595
  71.1 0.9 %copy-start.2 = (f32[136,128]{1,0:T(8,128)S(1)}, f32[136,128]{1,0:T(8,128)}, u32[]{:S(2)}) copy-start(f32[136,128]{1,0:T(8,128)} %join_2.1.mine) | copy-start | bytes 208900
  75.9 4.0 %collective-permute-start.11 = (bf16[16,1024]{1,0:T(8,128)(2,1)S(1)}, bf16[16,1024]{1,0:T(8,128)(2,1)S(1)}, u32[]{:S(2)}, u32[]{:S(2)}) collective-permute-start(bf16[16,1024]{1,0:T(8,128)(2,1)S(1)} %get-tuple-element.61), channel_id=1, source_target_pairs={{0,8},{8,0},{16,24},{24,16},{1,9},{9,1},{17,25},{25,17},{2,10},{10... | collective-permute-start | bytes 98312 | tf_op jit(solution)/shard_map/ppermute | solution.py:560
  76.5 3.9 %collective-permute-start.12 = (bf16[16,1024]{1,0:T(8,128)(2,1)S(1)}, bf16[16,1024]{1,0:T(8,128)(2,1)S(1)}, u32[]{:S(2)}, u32[]{:S(2)}) collective-permute-start(bf16[16,1024]{1,0:T(8,128)(2,1)S(1)} %get-tuple-element.62), channel_id=1, source_target_pairs={{0,16},{8,24},{16,0},{24,8},{1,17},{9,25},{17,1},{25,9},{2,18},{10... | collective-permute-start | bytes 98312 | tf_op jit(solution)/shard_map/ppermute | solution.py:560
  77.1 4.8 %collective-permute-start.13 = (bf16[16,1024]{1,0:T(8,128)(2,1)S(1)}, bf16[16,1024]{1,0:T(8,128)(2,1)S(1)}, u32[]{:S(2)}, u32[]{:S(2)}) collective-permute-start(bf16[16,1024]{1,0:T(8,128)(2,1)S(1)} %get-tuple-element.63), channel_id=1, source_target_pairs={{0,24},{8,16},{16,8},{24,0},{1,25},{9,17},{17,9},{25,1},{2,26},{10... | collective-permute-start | bytes 98312 | tf_op jit(solution)/shard_map/ppermute | solution.py:560
